TPU v7x, 32 devices: a whole 2x2x4 slice. The times are simulated.
32 devices in a mesh: groups: 2 (over x), cell: 16 (over z, y, core).
Axes of the slice: x: 2, y: 2, z: 4, core: 2. Of those that a mesh axis runs over, the one named last changes fastest.
Arguments:
- features: bfloat16 [256, 512, 128], P(('groups', 'cell')), parts along dimension 0, may hold values from -6 to 6
- neighbour_table: int32 [256, 26], P(('groups', 'cell')), parts along dimension 0, may hold values from 0 to 24
- send_lists: int32 [32, 4, 4], P(('groups', 'cell')), parts along dimension 0, may hold values from 0 to 7
- coarse_target: int32 [256], P('groups'), parts along dimension 0, may hold values from 0 to 31, as said below
- conv_weight: bfloat16 [3456, 128], replicated, may hold values from -0.109375 to 0.109375
- norm_gain: float32 [128], replicated, may hold values from 0.1 to 1.9
- norm_shift: float32 [128], replicated, may hold values from -3 to 3
- reduce_weight_matrix: bfloat16 [1024, 128], replicated, may hold values from -0.25 to 0.25
Outputs:
- fine_output_features: bfloat16 [256, 512, 128], P(('groups', 'cell')), parts along dimension 0
- coarse_out: bfloat16 [64, 512, 128], P(('groups', 'cell')), parts along dimension 0
There are 2 independent parts, one for each index of `groups`. A program takes and returns all parts, laid end to end along the dimension named above; an argument that names none is the same for every part. Nothing has to cross between parts.
Inputs may be any that keep to these rules, and one draw needn't show every extreme that they name: `neighbour_table`: the value 8 + 4 * 4 marks an empty neighbour; smaller values are local blocks, then halo slots. `coarse_target`: within each pair of devices 2m and 2m + 1 the values of their 16 blocks are distinct.
All inputs are finite; a program needn't handle non-finite values.
Results may differ from a plain program's by a relative error of at most 0.005.
Values may be sent and summed in bfloat16 or wider, within the bound.
A program may use at most 64 MiB of HBM per device.

v0:
```python
import jax
import jax.numpy as jnp
from jax import lax
from jax.sharding import PartitionSpec as P

OFFSETS = (1, -1, 2, -2)


def shifted(block, axis, distance):
    devices = range(lax.axis_size(axis))
    route = [(i - distance, i) for i in devices if i - distance in devices]
    return lax.ppermute(block, axis, route)


def shortened(x):
    return jax.tree.map(lambda a: a.astype(jnp.bfloat16) if a.dtype == jnp.float32 else a, x)


def swapped(block, axis, stride):
    count = lax.axis_size(axis)
    route = []
    for low in range(count):
        high = low | 1 << stride
        if high != low and high < count:
            route += [(low, high), (high, low)]
    return lax.ppermute(block, axis, route)


def take_slab(block, offset, device_dimension):
    if offset == -1:
        return lax.slice_in_dim(block, 7, 8, axis=device_dimension)
    if offset == 1:
        return lax.slice_in_dim(block, 0, 1, axis=device_dimension)
    return block


def slab_tables(extended, channel_total):
    cubes = extended.reshape(extended.shape[0], 8, 8, 8, channel_total)
    tables = []
    for shift_x in (-1, 0, 1):
        for shift_y in (-1, 0, 1):
            for shift_z in (-1, 0, 1):
                piece = take_slab(cubes, shift_x, 1)
                piece = take_slab(piece, shift_y, 2)
                piece = take_slab(piece, shift_z, 3)
                tables.append(piece)
    return tables


def conv_pieces(tables, ids, conv_weight, channel_total):
    planes = []
    for shift_x in (-1, 0, 1):
        rows_list = []
        for shift_y in (-1, 0, 1):
            cols_list = []
            for shift_z in (-1, 0, 1):
                number = (shift_x + 1) * 9 + (shift_y + 1) * 3 + (shift_z + 1)
                cols_list.append(tables[number][ids[number]])
            rows_list.append(jnp.concatenate(cols_list, axis=2))
        planes.append(jnp.concatenate(rows_list, axis=1))
    padded_cube = jnp.concatenate(planes, axis=0)
    columns = []
    for shift_x in (-1, 0, 1):
        for shift_y in (-1, 0, 1):
            for shift_z in (-1, 0, 1):
                window = padded_cube[
                    1 + shift_x : 9 + shift_x, 1 + shift_y : 9 + shift_y, 1 + shift_z : 9 + shift_z
                ]
                columns.append(window.reshape(512, channel_total))
    stack_cols = jnp.concatenate(columns, axis=1)
    return jnp.dot(stack_cols, conv_weight, preferred_element_type=jnp.float32)


def coarsen_blocks(fine_features, reduce_weight_matrix, channel_total):
    count = fine_features.shape[0]
    parts = fine_features.reshape(count, 4, 2, 4, 2, 4, 2, channel_total)
    parts = jnp.transpose(parts, (0, 1, 3, 5, 2, 4, 6, 7)).reshape(count, 64, 8 * channel_total)
    return jnp.einsum(
        "bvc,co->bvo", parts, reduce_weight_matrix, preferred_element_type=jnp.float32
    ).astype(jnp.bfloat16)


def per_device(
    features,
    neighbour_table,
    send_lists,
    coarse_target,
    conv_weight,
    norm_gain,
    norm_shift,
    reduce_weight_matrix,
):
    blocks_here = features.shape[0]
    channel_total = features.shape[2]
    myself = lax.axis_index("cell")
    own_lists = send_lists[0]
    received = []
    for number, distance in enumerate(OFFSETS):
        outgoing = jnp.take(features, own_lists[number], axis=0)
        received.append(shifted(outgoing, "cell", distance))
    extended = jnp.concatenate(
        [features] + received + [jnp.zeros((1, 512, channel_total), jnp.bfloat16)], axis=0
    )
    tables = slab_tables(extended, channel_total)
    self_id = jnp.arange(blocks_here, dtype=jnp.int32)[:, None]
    full_id = jnp.concatenate([neighbour_table[:, :13], self_id, neighbour_table[:, 13:]], axis=1)

    def one_block(ids):
        conv = conv_pieces(tables, ids, conv_weight, channel_total)
        return jnp.maximum(conv * norm_gain[None, :] + norm_shift[None, :], 0.0).astype(
            jnp.bfloat16
        )

    fine_output_features = lax.map(one_block, full_id)
    partner_fine_features = jax.tree.map(
        lambda part, own: part.astype(own.dtype),
        swapped(shortened(fine_output_features), "cell", 0),
        fine_output_features,
    )
    octant_list = coarsen_blocks(
        jnp.concatenate([fine_output_features, partner_fine_features], axis=0),
        reduce_weight_matrix,
        channel_total,
    )
    partner = jnp.bitwise_xor(myself, 1)
    own_target = lax.dynamic_slice_in_dim(coarse_target, myself * blocks_here, blocks_here)
    partner_target = lax.dynamic_slice_in_dim(coarse_target, partner * blocks_here, blocks_here)
    targets = jnp.concatenate([own_target, partner_target], axis=0)
    slots_here = blocks_here // 4
    owner_mine = targets // (8 * slots_here) == myself % 2
    slot_rows = targets % (8 * slots_here)
    selector = (
        slot_rows[None, :] == jnp.arange(8 * slots_here, dtype=jnp.int32)[:, None]
    ) & owner_mine[None, :]
    coarse_rows = jnp.dot(
        selector.astype(jnp.bfloat16),
        octant_list.reshape(2 * blocks_here, 64 * channel_total),
        preferred_element_type=jnp.float32,
    )
    coarse = coarse_rows.astype(jnp.bfloat16).reshape(slots_here, 2, 2, 2, 4, 4, 4, channel_total)
    coarse = jnp.transpose(coarse, (0, 1, 4, 2, 5, 3, 6, 7)).reshape(slots_here, 512, channel_total)
    return (fine_output_features, coarse)


def solution(mesh):
    return jax.shard_map(
        per_device,
        mesh=mesh,
        in_specs=(
            P(("groups", "cell"), None, None),
            P(("groups", "cell"), None),
            P(("groups", "cell"), None, None),
            P("groups"),
            P(),
            P(),
            P(),
            P(),
        ),
        out_specs=(P(("groups", "cell"), None, None), P(("groups", "cell"), None, None)),
        check_vma=False,
    )
```

profile of v0, /device:TPU:11, one launch (start us, length us, event | category | flops | bytes accessed | tf_op | source)
XLA Modules:
  0.0 668.4 jit_solution(3893703375818675499)
XLA Ops:
  1.5 1.9 gather_fusion
  4.3 3.7 collective-permute-start
  8.0 1.9 gather_fusion.1
  10.9 1.9 collective-permute-start.1
  14.4 3.1 collective-permute-start.2
  19.1 3.0 collective-permute-start.3
  23.5 11.0 %collective-permute-done.1 = bf16[4,512,128]{2,1,0:T(8,128)(2,1)} collective-permute-done((bf16[4,512,128]{2,1,0:T(8,128)(2,1)}, bf16[4,512,128]{2,1,0:T(8,128)(2,1)}, u32[]{:S(2)}, u32[]{:S(2)}) %collective-permute-start.1) | collective-permute-done | bytes 524320 | tf_op jit(solution)/shard_map/ppermute | solution.py:12
  35.6 8.6 %collective-permute-done.2 = bf16[4,512,128]{2,1,0:T(8,128)(2,1)} collective-permute-done((bf16[4,512,128]{2,1,0:T(8,128)(2,1)}, bf16[4,512,128]{2,1,0:T(8,128)(2,1)}, u32[]{:S(2)}, u32[]{:S(2)}) %collective-permute-start.2) | collective-permute-done | bytes 524320 | tf_op jit(solution)/shard_map/ppermute | solution.py:12
  55.0 602.0 %while.10 = (s32[]{:T(128)}, bf16[8,512,128]{2,1,0:T(8,128)(2,1)S(1)}, s32[8,27]{1,0:T(8,128)S(1)}, bf16[25,1,1,1,128]{4,3,2,1,0:T(2,128)(2,1)}, bf16[25,1,1,8,1...) while((s32[]{:T(128)}, ...), condition=%wide.region_1.3_spmd, body=%wide.region_0.0_spmd.sunk | while | flops 463048800 | bytes 41703108 | solution.py:114
  103.6 1.7 copy-done.6
  127.0 3.1 fusion.94
  178.8 1.7 copy-done.6
  202.2 3.1 fusion.94
  254.1 1.7 copy-done.6
  277.5 3.1 fusion.94
  352.8 3.1 fusion.94
  404.6 1.7 copy-done.6
  428.1 3.1 fusion.94
  503.3 3.1 fusion.94
  578.6 3.1 fusion.94
  630.4 1.7 copy-done.6
  653.9 3.1 fusion.94
  659.9 3.2 copy.58
  663.2 3.2 reshape.286
  (700 shorter events, 188.7 us)
Async XLA Ops:
  0.6 665.8 %copy-start = (bf16[1024,128]{1,0:T(8,128)(2,1)S(1)}, bf16[1024,128]{1,0:T(8,128)(2,1)}, u32[]{:S(2)}) copy-start(bf16[1024,128]{1,0:T(8,128)(2,1)} %param.19) | copy-start | bytes 786436
  3.4 18.7 %copy-start.7 = (s32[8,26]{1,0:T(8,128)S(1)}, s32[8,26]{1,0:T(8,128)}, u32[]{:S(2)}) copy-start(s32[8,26]{1,0:T(8,128)} %param.13) | copy-start | bytes 2500
  4.3 18.1 %collective-permute-start = (bf16[4,512,128]{2,1,0:T(8,128)(2,1)}, bf16[4,512,128]{2,1,0:T(8,128)(2,1)}, u32[]{:S(2)}, u32[]{:S(2)}) collective-permute-start(bf16[4,512,128]{2,1,0:T(8,128)(2,1)} %broadcast_select_fusion.3), channel_id=1, source_target_pairs={{0,1},{1,2},{2,3},{3,4},{4,5},{5,6},{6,7},{7,8},{8,9},{9,10},{10,1... | collective-permute-start | bytes 1572872 | tf_op jit(solution)/shard_map/ppermute | solution.py:12
  10.9 23.7 %collective-permute-start.1 = (bf16[4,512,128]{2,1,0:T(8,128)(2,1)}, bf16[4,512,128]{2,1,0:T(8,128)(2,1)}, u32[]{:S(2)}, u32[]{:S(2)}) collective-permute-start(bf16[4,512,128]{2,1,0:T(8,128)(2,1)} %broadcast_select_fusion.2), channel_id=1, source_target_pairs={{1,0},{2,1},{3,2},{4,3},{5,4},{6,5},{7,6},{8,7},{9,8},{10,9},{11,1... | collective-permute-start | bytes 1572872 | tf_op jit(solution)/shard_map/ppermute | solution.py:12
  14.4 29.9 %collective-permute-start.2 = (bf16[4,512,128]{2,1,0:T(8,128)(2,1)}, bf16[4,512,128]{2,1,0:T(8,128)(2,1)}, u32[]{:S(2)}, u32[]{:S(2)}) collective-permute-start(bf16[4,512,128]{2,1,0:T(8,128)(2,1)} %broadcast_select_fusion.1), channel_id=1, source_target_pairs={{0,2},{1,3},{2,4},{3,5},{4,6},{5,7},{6,8},{7,9},{8,10},{9,11},{10,... | collective-permute-start | bytes 1572872 | tf_op jit(solution)/shard_map/ppermute | solution.py:12
  19.1 26.3 %collective-permute-start.3 = (bf16[4,512,128]{2,1,0:T(8,128)(2,1)}, bf16[4,512,128]{2,1,0:T(8,128)(2,1)S(1)}, u32[]{:S(2)}, u32[]{:S(2)}) collective-permute-start(bf16[4,512,128]{2,1,0:T(8,128)(2,1)} %broadcast_select_fusion), channel_id=1, source_target_pairs={{2,0},{3,1},{4,2},{5,3},{6,4},{7,5},{8,6},{9,7},{10,8},{11,9},{12,... | collective-permute-start | bytes 1572872 | tf_op jit(solution)/shard_map/ppermute | solution.py:12
  103.3 23.6 %copy-start.11 = (f32[128]{0:T(128)S(1)}, f32[128]{0:T(128)}, u32[]{:S(2)}) copy-start(f32[128]{0:T(128)} %get-tuple-element.870) | copy-start | bytes 1540 | tf_op jit(solution)/shard_map/while
  103.4 23.6 %copy-start.12 = (f32[128]{0:T(128)S(1)}, f32[128]{0:T(128)}, u32[]{:S(2)}) copy-start(f32[128]{0:T(128)} %get-tuple-element.871) | copy-start | bytes 1540 | tf_op jit(solution)/shard_map/while
  130.1 13.9 %copy-start.4 = (bf16[25,8,1,8,128]{4,3,1,2,0:T(8,128)(2,1)}, bf16[25,8,1,8,128]{4,3,1,2,0:T(8,128)(2,1)S(1)}, u32[]{:S(2)}) copy-start(bf16[25,8,1,8,128]{4,3,1,2,0:T(8,128)(2,1)S(1)} %get-tuple-element.858) | copy-start | bytes 1228804 | tf_op jit(solution)/shard_map/while
  178.6 23.6 %copy-start.11 = (f32[128]{0:T(128)S(1)}, f32[128]{0:T(128)}, u32[]{:S(2)}) copy-start(f32[128]{0:T(128)} %get-tuple-element.870) | copy-start | bytes 1540 | tf_op jit(solution)/shard_map/while
  178.6 23.6 %copy-start.12 = (f32[128]{0:T(128)S(1)}, f32[128]{0:T(128)}, u32[]{:S(2)}) copy-start(f32[128]{0:T(128)} %get-tuple-element.871) | copy-start | bytes 1540 | tf_op jit(solution)/shard_map/while
  253.8 23.7 %copy-start.11 = (f32[128]{0:T(128)S(1)}, f32[128]{0:T(128)}, u32[]{:S(2)}) copy-start(f32[128]{0:T(128)} %get-tuple-element.870) | copy-start | bytes 1540 | tf_op jit(solution)/shard_map/while
  253.8 23.7 %copy-start.12 = (f32[128]{0:T(128)S(1)}, f32[128]{0:T(128)}, u32[]{:S(2)}) copy-start(f32[128]{0:T(128)} %get-tuple-element.871) | copy-start | bytes 1540 | tf_op jit(solution)/shard_map/while
  329.1 23.7 %copy-start.11 = (f32[128]{0:T(128)S(1)}, f32[128]{0:T(128)}, u32[]{:S(2)}) copy-start(f32[128]{0:T(128)} %get-tuple-element.870) | copy-start | bytes 1540 | tf_op jit(solution)/shard_map/while
  329.1 23.7 %copy-start.12 = (f32[128]{0:T(128)S(1)}, f32[128]{0:T(128)}, u32[]{:S(2)}) copy-start(f32[128]{0:T(128)} %get-tuple-element.871) | copy-start | bytes 1540 | tf_op jit(solution)/shard_map/while
  404.4 23.7 %copy-start.11 = (f32[128]{0:T(128)S(1)}, f32[128]{0:T(128)}, u32[]{:S(2)}) copy-start(f32[128]{0:T(128)} %get-tuple-element.870) | copy-start | bytes 1540 | tf_op jit(solution)/shard_map/while
  404.4 23.7 %copy-start.12 = (f32[128]{0:T(128)S(1)}, f32[128]{0:T(128)}, u32[]{:S(2)}) copy-start(f32[128]{0:T(128)} %get-tuple-element.871) | copy-start | bytes 1540 | tf_op jit(solution)/shard_map/while
  479.7 23.6 %copy-start.11 = (f32[128]{0:T(128)S(1)}, f32[128]{0:T(128)}, u32[]{:S(2)}) copy-start(f32[128]{0:T(128)} %get-tuple-element.870) | copy-start | bytes 1540 | tf_op jit(solution)/shard_map/while
  479.7 23.6 %copy-start.12 = (f32[128]{0:T(128)S(1)}, f32[128]{0:T(128)}, u32[]{:S(2)}) copy-start(f32[128]{0:T(128)} %get-tuple-element.871) | copy-start | bytes 1540 | tf_op jit(solution)/shard_map/while
  554.9 23.7 %copy-start.11 = (f32[128]{0:T(128)S(1)}, f32[128]{0:T(128)}, u32[]{:S(2)}) copy-start(f32[128]{0:T(128)} %get-tuple-element.870) | copy-start | bytes 1540 | tf_op jit(solution)/shard_map/while
  554.9 23.7 %copy-start.12 = (f32[128]{0:T(128)S(1)}, f32[128]{0:T(128)}, u32[]{:S(2)}) copy-start(f32[128]{0:T(128)} %get-tuple-element.871) | copy-start | bytes 1540 | tf_op jit(solution)/shard_map/while
  630.2 23.7 %copy-start.11 = (f32[128]{0:T(128)S(1)}, f32[128]{0:T(128)}, u32[]{:S(2)}) copy-start(f32[128]{0:T(128)} %get-tuple-element.870) | copy-start | bytes 1540 | tf_op jit(solution)/shard_map/while
  630.2 23.7 %copy-start.12 = (f32[128]{0:T(128)S(1)}, f32[128]{0:T(128)}, u32[]{:S(2)}) copy-start(f32[128]{0:T(128)} %get-tuple-element.871) | copy-start | bytes 1540 | tf_op jit(solution)/shard_map/while
  657.0 2.7 collective-permute-start.4
  (50 other events, 367.7 us)
where the time goes:
time: 679 us; the launch traced here: 668 us
  loops' own time  404 us (59%)
  local copies, waits for them, and re-layouts  193 us (28%)
  matrix products  25.9 us (4%)
  waiting for transfers between devices  21.2 us (3%)
  other arithmetic  12 us (2%)
  starting transfers between devices  12 us (2%)
    another operation x1, loops' own time, per_device(): fine_output_features = lax.map(one_block, full_id)  404 us
    squeeze x200, local copies, waits for them, and re-layouts, conv_pieces(): cols_list.append(tables[number][ids[number]])  75.2 us
    while x336, local copies, waits for them, and re-layouts  62.5 us
    dot_general x8, matrix products, conv_pieces(): return jnp.dot(stack_cols, conv_weight, preferred_element_type=jnp.float32)  25 us
    ppermute x4, waiting for transfers between devices, shifted(): return lax.ppermute(block, axis, route)  19.7 us
  transfers between devices with their start and end apart: 5, of which 3 were waited for; matrix products, arithmetic and copies ran while one was open for 2% of the time, Pallas kernels for 0%

commit v1 on v0

v1 whole, which is shorter than its diff:
```python
import jax
import jax.numpy as jnp
import numpy as np
from jax import lax
from jax.experimental import pallas as pl
from jax.experimental.pallas import tpu as pltpu
from jax.sharding import PartitionSpec as P

OFFSETS = (1, -1, 2, -2)


def shifted(block, axis, distance):
    devices = range(lax.axis_size(axis))
    route = [(i - distance, i) for i in devices if i - distance in devices]
    return lax.ppermute(block, axis, route)


def swapped(block, axis):
    count = lax.axis_size(axis)
    return lax.ppermute(block, axis, [(i, i ^ 1) for i in range(count)])


def octant_order():
    order = np.zeros((128, 128), np.float32)
    for p in range(8):
        px, py, pz = p // 4, p // 2 % 2, p % 2
        for b in range(4):
            for c in range(4):
                order[p * 16 + b * 4 + c, px * 64 + (2 * b + py) * 8 + 2 * c + pz] = 1
    return jnp.asarray(order, jnp.bfloat16)


def coarse_order():
    order = np.zeros((64, 64), np.float32)
    for q in range(4):
        qy, qz = q // 2, q % 2
        for b in range(4):
            for c in range(4):
                order[(4 * qy + b) * 8 + 4 * qz + c, q * 16 + b * 4 + c] = 1
    return jnp.asarray(order, jnp.bfloat16)


def pick_kernel(lists, feats, out0, out1, out2, out3, sems):
    copies = []
    for i, out in enumerate((out0, out1, out2, out3)):
        for slot in range(out.shape[0]):
            copies.append(
                pltpu.make_async_copy(
                    feats.at[lists[i, slot]], out.at[slot], sems.at[i * out.shape[0] + slot]
                )
            )
    for copy in copies:
        copy.start()
    for copy in copies:
        copy.wait()


def fill_columns(g, ids, ext, cols):
    z = lax.broadcasted_iota(jnp.int32, (8, 8, 128), 1)

    def band(number, plane, oy):
        low, size = {-1: (48, 16), 0: (0, 64), 1: (0, 16)}[oy]
        rows = ext[ids[g, number], pl.ds(plane * 64 + low, size), :].astype(jnp.float32)
        rows = rows.reshape(size // 8, 8, 128)
        return {-1: rows[1:], 0: rows, 1: rows[:1]}[oy]

    def plane_of(place, ox, plane):
        bands = []
        for oy in (-1, 0, 1):
            first = 9 * (ox + 1) + 3 * (oy + 1)
            low, mid, high = (band(first + i, plane, oy) for i in range(3))
            mask = z[: mid.shape[0]]
            bands.append(
                (
                    pltpu.roll(jnp.where(mask == 7, low, mid), 1, 1),
                    mid,
                    pltpu.roll(jnp.where(mask == 0, high, mid), 7, 1),
                )
            )
        for kz in range(3):
            whole = jnp.concatenate([bands[0][kz], bands[1][kz], bands[2][kz]], axis=0)
            for ky in range(3):
                column = 3 * ky + kz
                cols[place, :, column * 128 : (column + 1) * 128] = (
                    whole[ky : ky + 8].reshape(64, 128).astype(jnp.bfloat16)
                )

    plane_of(0, -1, 7)
    for plane in range(8):
        plane_of(plane + 1, 0, plane)
    plane_of(9, 1, 0)


def conv_kernel(
    ids, feats, from0, from1, from2, from3, weight, gain, shift, reduce, order,
    fine, octant, ext, cols, grouped, sems,
):
    g = pl.program_id(0)
    blocks, slots = feats.shape[0], from0.shape[0]

    @pl.when(g == 0)
    def _():
        copies = [pltpu.make_async_copy(feats, ext.at[pl.ds(0, blocks)], sems.at[0])]
        for i, part in enumerate((from0, from1, from2, from3)):
            copies.append(
                pltpu.make_async_copy(
                    part, ext.at[pl.ds(blocks + i * slots, slots)], sems.at[i + 1]
                )
            )
        for copy in copies:
            copy.start()
        ext[blocks + 4 * slots] = jnp.zeros(ext.shape[1:], ext.dtype)
        for copy in copies:
            copy.wait()

    fill_columns(g, ids, ext, cols)
    total = None
    for kx in range(3):
        term = jnp.dot(
            cols[kx : kx + 8].reshape(512, 1152),
            weight[kx * 1152 : (kx + 1) * 1152],
            preferred_element_type=jnp.float32,
        )
        total = term if total is None else total + term
    out = jnp.maximum(total * gain[...] + shift[...], 0.0).astype(jnp.bfloat16)
    fine[0] = out
    for a in range(4):
        rows = jnp.dot(
            order[...], out[a * 128 : (a + 1) * 128], preferred_element_type=jnp.float32
        ).astype(jnp.bfloat16)
        for p in range(8):
            grouped[a * 16 : (a + 1) * 16, p * 128 : (p + 1) * 128] = rows[p * 16 : (p + 1) * 16]
    octant[0] = jnp.dot(
        grouped[...], reduce[...], preferred_element_type=jnp.float32
    ).astype(jnp.bfloat16)


def place_kernel(source, mine, other, order, coarse, rows, stack):
    count = mine.shape[0]
    rows[:count] = mine[...]
    rows[count : 2 * count] = other[...]
    rows[2 * count] = jnp.zeros(rows.shape[1:], rows.dtype)
    for slot in range(coarse.shape[0]):
        for qx in range(2):
            for a in range(4):
                for q in range(4):
                    stack[q * 16 : (q + 1) * 16] = rows[
                        source[slot * 8 + qx * 4 + q], a * 16 : (a + 1) * 16
                    ]
                start = (4 * qx + a) * 64
                coarse[slot, start : start + 64] = jnp.dot(
                    order[...], stack[...], preferred_element_type=jnp.float32
                ).astype(jnp.bfloat16)


def per_device(
    features,
    neighbour_table,
    send_lists,
    coarse_target,
    conv_weight,
    norm_gain,
    norm_shift,
    reduce_weight_matrix,
):
    blocks = features.shape[0]
    slots = send_lists.shape[2]
    channels = features.shape[2]
    myself = lax.axis_index("cell")
    vmem = pl.BlockSpec(memory_space=pltpu.VMEM)
    smem = pl.BlockSpec(memory_space=pltpu.SMEM)
    hbm = pl.BlockSpec(memory_space=pl.ANY)
    outgoing = pl.pallas_call(
        pick_kernel,
        in_specs=[smem, hbm],
        out_specs=[hbm] * 4,
        out_shape=[jax.ShapeDtypeStruct((slots, 512, channels), jnp.bfloat16)] * 4,
        scratch_shapes=[pltpu.SemaphoreType.DMA((4 * slots,))],
    )(send_lists[0], features)
    received = [shifted(part, "cell", d) for part, d in zip(outgoing, OFFSETS)]
    self_id = jnp.arange(blocks, dtype=jnp.int32)[:, None]
    ids = jnp.concatenate([neighbour_table[:, :13], self_id, neighbour_table[:, 13:]], axis=1)
    fine, octants = pl.pallas_call(
        conv_kernel,
        grid_spec=pltpu.PrefetchScalarGridSpec(
            num_scalar_prefetch=1,
            grid=(blocks,),
            in_specs=[hbm] * 5 + [vmem] * 5,
            out_specs=[
                pl.BlockSpec((1, 512, channels), lambda g, ids: (g, 0, 0)),
                pl.BlockSpec((1, 64, channels), lambda g, ids: (g, 0, 0)),
            ],
            scratch_shapes=[
                pltpu.VMEM((blocks + 4 * slots + 1, 512, channels), jnp.bfloat16),
                pltpu.VMEM((10, 64, 9 * channels), jnp.bfloat16),
                pltpu.VMEM((64, 8 * channels), jnp.bfloat16),
                pltpu.SemaphoreType.DMA((5,)),
            ],
        ),
        out_shape=[
            jax.ShapeDtypeStruct((blocks, 512, channels), jnp.bfloat16),
            jax.ShapeDtypeStruct((blocks, 64, channels), jnp.bfloat16),
        ],
        compiler_params=pltpu.CompilerParams(vmem_limit_bytes=40 * 1024 * 1024),
    )(
        ids, features, *received, conv_weight, norm_gain[None], norm_shift[None],
        reduce_weight_matrix, octant_order(),
    )
    partner_octants = swapped(octants, "cell")
    partner = jnp.bitwise_xor(myself, 1)
    targets = jnp.concatenate(
        [
            lax.dynamic_slice_in_dim(coarse_target, myself * blocks, blocks),
            lax.dynamic_slice_in_dim(coarse_target, partner * blocks, blocks),
        ]
    )
    coarse_slots = blocks // 4
    wanted = (myself % 2) * 8 * coarse_slots + jnp.arange(8 * coarse_slots, dtype=jnp.int32)
    hit = targets[None, :] == wanted[:, None]
    source = jnp.min(jnp.where(hit, jnp.arange(2 * blocks, dtype=jnp.int32), 2 * blocks), axis=1)
    coarse = pl.pallas_call(
        place_kernel,
        in_specs=[smem, vmem, vmem, vmem],
        out_specs=vmem,
        out_shape=jax.ShapeDtypeStruct((coarse_slots, 512, channels), jnp.bfloat16),
        scratch_shapes=[
            pltpu.VMEM((2 * blocks + 1, 64, channels), jnp.bfloat16),
            pltpu.VMEM((64, channels), jnp.bfloat16),
        ],
        compiler_params=pltpu.CompilerParams(vmem_limit_bytes=16 * 1024 * 1024),
    )(source.astype(jnp.int32), octants, partner_octants, coarse_order())
    return (fine, coarse)


def solution(mesh):
    return jax.shard_map(
        per_device,
        mesh=mesh,
        in_specs=(
            P(("groups", "cell"), None, None),
            P(("groups", "cell"), None),
            P(("groups", "cell"), None, None),
            P("groups"),
            P(),
            P(),
            P(),
            P(),
        ),
        out_specs=(P(("groups", "cell"), None, None), P(("groups", "cell"), None, None)),
        check_vma=False,
    )
```

time: 679 us -> 126 us (0.19); the launches traced: 668 us -> 126 us
  loops' own time: 404 us -> 0 us
  local copies, waits for them, and re-layouts: 193 us -> 3.56 us
  Pallas kernels: 0 us -> 80.7 us
  matrix products: 25.9 us -> 0 us
  other arithmetic: 12 us -> 0.34 us
    another operation x1 -> x0, loops' own time: 404 us -> none  [per_device(): fine_output_features = lax.map(one_block, full_id)]
    pallas_call x0 -> x3, Pallas kernels: none -> 80.7 us  [the longest x1 65.6 us: per_device(): pl.pallas_call(pick_kernel, in_specs=[smem, hbm], out_specs=[hbm] * 4, ou...]
    squeeze x200 -> x0, local copies, waits for them, and re-layouts: 75.2 us -> none  [conv_pieces(): cols_list.append(tables[number][ids[number]])]
    while x338 -> x0, local copies, waits for them, and re-layouts: 63.7 us -> none
    dot_general x10 -> x0, matrix products: 25.9 us -> none  [the longest x8 25 us: conv_pieces(): return jnp.dot(stack_cols, conv_weight, preferred_element_type=jnp.float32)]
    slice x54 -> x0, local copies, waits for them, and re-layouts: 19.8 us -> none  [the longest x16 11.4 us: conv_pieces(): cols_list.append(tables[number][ids[number]])]
    dynamic_slice x17 -> x1, local copies, waits for them, and re-layouts: 8.24 us -> 0.08 us  [per_device(): lax.dynamic_slice_in_dim(coarse_target, myself * blocks, blocks)]
    concatenate x41 -> x1, other arithmetic: 7.29 us -> 0.07 us  [per_device(): jnp.concatenate([lax.dynamic_slice_in_dim(coarse_target, myself * blocks,...]
  transfers between devices with their start and end apart: 5 -> 5, of which waited for: 3 -> 4; matrix products, arithmetic and copies ran while one was open for 2% -> 0% of each run, Pallas kernels for 0% -> 0%
where the time goes in v1:
time: 126 us
  Pallas kernels  80.7 us (64%)
  waiting for transfers between devices  26.2 us (21%)
  starting transfers between devices  14 us (11%)
  local copies, waits for them, and re-layouts  3.56 us (3%)
    pallas_call x1, Pallas kernels, per_device(): pl.pallas_call(pick_kernel, in_specs=[smem, hbm], out_specs=[hbm] * 4, ou...  65.6 us
    ppermute x4, waiting for transfers between devices, shifted(): return lax.ppermute(block, axis, route)  25.5 us
    pallas_call x1, Pallas kernels, per_device(): pl.pallas_call(conv_kernel, grid_spec=pltpu.PrefetchScalarGridSpec(num_sc...  13.6 us
    ppermute x4, starting transfers between devices, shifted(): return lax.ppermute(block, axis, route)  11.8 us
    unnamed x18, local copies, waits for them, and re-layouts  3.41 us
  transfers between devices with their start and end apart: 5, of which 4 were waited for; matrix products, arithmetic and copies ran while one was open for 0% of the time, Pallas kernels for 0%

profile of v1, /device:TPU:11, one launch (start us, length us, event | category | flops | bytes accessed | tf_op | source)
XLA Modules:
  0.0 125.6 jit_solution(2559384441909849932)
XLA Ops:
  0.6 65.6 %shard_map.113 = (bf16[4,512,128]{2,1,0:T(8,128)(2,1)}, bf16[4,512,128]{2,1,0:T(8,128)(2,1)}, bf16[4,512,128]{2,1,0:T(8,128)(2,1)}, bf16[4,512,128]{2,1,0:T(8,128)(2,1)}) custom-call(s32[4,4]{1,0:T(4,128)} %bitcast.5, bf16[8,512,128]{2,1,0:T(8,128)(2,1)} %feats.3), custom_call_target="tpu_custom_call" | custom-call | tf_op jit(solution)/shard_map/pallas_call | solution.py:173
  66.2 3.7 %collective-permute-start = (bf16[4,512,128]{2,1,0:T(8,128)(2,1)}, bf16[4,512,128]{2,1,0:T(8,128)(2,1)S(1)}, u32[]{:S(2)}, u32[]{:S(2)}) collective-permute-start(bf16[4,512,128]{2,1,0:T(8,128)(2,1)} %get-tuple-element.8), channel_id=1, source_target_pairs={{0,1},{1,2},{2,3},{3,4},{4,5},{5,6},{6,7},{7,8},{8,9},{9,10},{10,1... | collective-permute-start | bytes 1572872 | tf_op jit(solution)/shard_map/ppermute | solution.py:15
  70.0 1.9 %collective-permute-start.1 = (bf16[4,512,128]{2,1,0:T(8,128)(2,1)}, bf16[4,512,128]{2,1,0:T(8,128)(2,1)S(1)}, u32[]{:S(2)}, u32[]{:S(2)}) collective-permute-start(bf16[4,512,128]{2,1,0:T(8,128)(2,1)} %get-tuple-element.9), channel_id=1, source_target_pairs={{1,0},{2,1},{3,2},{4,3},{5,4},{6,5},{7,6},{8,7},{9,8},{10,9},{11,1... | collective-permute-start | bytes 1572872 | tf_op jit(solution)/shard_map/ppermute | solution.py:15
  71.9 3.1 %collective-permute-start.2 = (bf16[4,512,128]{2,1,0:T(8,128)(2,1)}, bf16[4,512,128]{2,1,0:T(8,128)(2,1)S(1)}, u32[]{:S(2)}, u32[]{:S(2)}) collective-permute-start(bf16[4,512,128]{2,1,0:T(8,128)(2,1)} %get-tuple-element.10), channel_id=1, source_target_pairs={{0,2},{1,3},{2,4},{3,5},{4,6},{5,7},{6,8},{7,9},{8,10},{9,11},{10,... | collective-permute-start | bytes 1572872 | tf_op jit(solution)/shard_map/ppermute | solution.py:15
  75.0 3.0 %collective-permute-start.3 = (bf16[4,512,128]{2,1,0:T(8,128)(2,1)}, bf16[4,512,128]{2,1,0:T(8,128)(2,1)S(1)}, u32[]{:S(2)}, u32[]{:S(2)}) collective-permute-start(bf16[4,512,128]{2,1,0:T(8,128)(2,1)} %get-tuple-element.11), channel_id=1, source_target_pairs={{2,0},{3,1},{4,2},{5,3},{6,4},{7,5},{8,6},{9,7},{10,8},{11,9},{12,... | collective-permute-start | bytes 1572872 | tf_op jit(solution)/shard_map/ppermute | solution.py:15
  78.1 0.0 copy-start.8
  78.1 0.0 copy-start.3
  78.1 0.6 copy-done.8
  78.8 0.1 fusion.1
  78.8 0.1 fusion
  78.9 0.1 pad_add_fusion.ids
  79.0 15.1 %collective-permute-done.from0 = bf16[4,512,128]{2,1,0:T(8,128)(2,1)S(1)} collective-permute-done((bf16[4,512,128]{2,1,0:T(8,128)(2,1)}, bf16[4,512,128]{2,1,0:T(8,128)(2,1)S(1)}, u32[]{:S(2)}, u32[]{:S(2)}) %collective-permute-start) | collective-permute-done | bytes 524320 | tf_op jit(solution)/shard_map/ppermute | solution.py:15
  94.1 6.2 %collective-permute-done.1.from1 = bf16[4,512,128]{2,1,0:T(8,128)(2,1)S(1)} collective-permute-done((bf16[4,512,128]{2,1,0:T(8,128)(2,1)}, bf16[4,512,128]{2,1,0:T(8,128)(2,1)S(1)}, u32[]{:S(2)}, u32[]{:S(2)}) %collective-permute-start.1) | collective-permute-done | bytes 524320 | tf_op jit(solution)/shard_map/ppermute | solution.py:15
  100.2 4.3 %collective-permute-done.2.from2 = bf16[4,512,128]{2,1,0:T(8,128)(2,1)S(1)} collective-permute-done((bf16[4,512,128]{2,1,0:T(8,128)(2,1)}, bf16[4,512,128]{2,1,0:T(8,128)(2,1)S(1)}, u32[]{:S(2)}, u32[]{:S(2)}) %collective-permute-start.2) | collective-permute-done | bytes 524320 | tf_op jit(solution)/shard_map/ppermute | solution.py:15
  104.5 0.6 copy-done.5
  105.1 0.0 copy-done.6
  105.2 1.2 copy-done.1
  106.3 0.9 copy-done.2
  107.3 13.6 %shard_map.114 = (bf16[8,512,128]{2,1,0:T(8,128)(2,1)}, bf16[8,64,128]{2,1,0:T(8,128)(2,1)S(1)}) custom-call(s32[8,27]{1,0:T(8,128)S(1)} %pad_add_fusion.ids, bf16[8,512,128]{2,1,0:T(8,128)(2,1)S(1)} %copy-done, bf16[4,512,128]{2,1,0:T(8,128)(2,1)S(1)} %collective-permute-done.from0, bf16[4,512,128]{2,1,0:T(8,128)(2,1)S(1)} %collective-permute-done.1.from1, ...), custom_call_target="tpu_custom_call" | custom-call | tf_op jit(solution)/shard_map/pallas_call | solution.py:183
  120.9 2.2 %collective-permute-start.4 = (bf16[8,64,128]{2,1,0:T(8,128)(2,1)S(1)}, bf16[8,64,128]{2,1,0:T(8,128)(2,1)S(1)}, u32[]{:S(2)}, u32[]{:S(2)}) collective-permute-start(bf16[8,64,128]{2,1,0:T(8,128)(2,1)S(1)} %get-tuple-element.13.mine), channel_id=1, source_target_pairs={{0,1},{1,0},{2,3},{3,2},{4,5},{5,4},{6,7},{7,6},{8,9},{9,8},{10,11... | collective-permute-start | bytes 393224 | tf_op jit(solution)/shard_map/ppermute | solution.py:20
  123.1 0.1 pad_add_fusion.1
  123.2 0.2 select_reduce_fusion.source
  123.4 0.7 collective-permute-done.4.other
  124.1 1.5 %shard_map.115 = bf16[2,512,128]{2,1,0:T(8,128)(2,1)} custom-call(s32[16]{0:T(128)S(1)} %select_reduce_fusion.source, bf16[8,64,128]{2,1,0:T(8,128)(2,1)S(1)} %get-tuple-element.13.mine, bf16[8,64,128]{2,1,0:T(8,128)(2,1)S(1)} %collective-permute-done.4.other, bf16[64,64]{1,0:T(8,128)(2,1)S(1)} %copy-done.4), custom_call_target="tpu_custom_call" | custom-call | tf_op jit(solution)/shard_map/pallas_call | solution.py:221
  (13 shorter events, 0.0 us)
Async XLA Ops:
  0.6 103.9 %copy-start = (bf16[8,512,128]{2,1,0:T(8,128)(2,1)S(1)}, bf16[8,512,128]{2,1,0:T(8,128)(2,1)}, u32[]{:S(2)}) copy-start(bf16[8,512,128]{2,1,0:T(8,128)(2,1)} %feats.3) | copy-start | bytes 3145732
  66.2 27.8 %collective-permute-start = (bf16[4,512,128]{2,1,0:T(8,128)(2,1)}, bf16[4,512,128]{2,1,0:T(8,128)(2,1)S(1)}, u32[]{:S(2)}, u32[]{:S(2)}) collective-permute-start(bf16[4,512,128]{2,1,0:T(8,128)(2,1)} %get-tuple-element.8), channel_id=1, source_target_pairs={{0,1},{1,2},{2,3},{3,4},{4,5},{5,6},{6,7},{7,8},{8,9},{9,10},{10,1... | collective-permute-start | bytes 1572872 | tf_op jit(solution)/shard_map/ppermute | solution.py:15
  70.0 30.3 %collective-permute-start.1 = (bf16[4,512,128]{2,1,0:T(8,128)(2,1)}, bf16[4,512,128]{2,1,0:T(8,128)(2,1)S(1)}, u32[]{:S(2)}, u32[]{:S(2)}) collective-permute-start(bf16[4,512,128]{2,1,0:T(8,128)(2,1)} %get-tuple-element.9), channel_id=1, source_target_pairs={{1,0},{2,1},{3,2},{4,3},{5,4},{6,5},{7,6},{8,7},{9,8},{10,9},{11,1... | collective-permute-start | bytes 1572872 | tf_op jit(solution)/shard_map/ppermute | solution.py:15
  71.9 32.6 %collective-permute-start.2 = (bf16[4,512,128]{2,1,0:T(8,128)(2,1)}, bf16[4,512,128]{2,1,0:T(8,128)(2,1)S(1)}, u32[]{:S(2)}, u32[]{:S(2)}) collective-permute-start(bf16[4,512,128]{2,1,0:T(8,128)(2,1)} %get-tuple-element.10), channel_id=1, source_target_pairs={{0,2},{1,3},{2,4},{3,5},{4,6},{5,7},{6,8},{7,9},{8,10},{9,11},{10,... | collective-permute-start | bytes 1572872 | tf_op jit(solution)/shard_map/ppermute | solution.py:15
  75.0 29.4 %collective-permute-start.3 = (bf16[4,512,128]{2,1,0:T(8,128)(2,1)}, bf16[4,512,128]{2,1,0:T(8,128)(2,1)S(1)}, u32[]{:S(2)}, u32[]{:S(2)}) collective-permute-start(bf16[4,512,128]{2,1,0:T(8,128)(2,1)} %get-tuple-element.11), channel_id=1, source_target_pairs={{2,0},{3,1},{4,2},{5,3},{6,4},{7,5},{8,6},{9,7},{10,8},{11,9},{12,... | collective-permute-start | bytes 1572872 | tf_op jit(solution)/shard_map/ppermute | solution.py:15
  78.1 0.7 copy-start.8
  78.1 0.7 copy-start.7
  78.1 26.4 %copy-start.3 = (bf16[128,128]{1,0:T(8,128)(2,1)S(1)}, bf16[128,128]{1,0:T(8,128)(2,1)}, u32[]{:S(2)}) copy-start(bf16[128,128]{1,0:T(8,128)(2,1)} %constant.32.clone.order) | copy-start | bytes 98308
  104.5 0.7 copy-start.5
  104.5 0.7 copy-start.6
  105.1 1.2 copy-start.1
  106.3 0.9 copy-start.2
  107.3 16.8 %copy-start.4 = (bf16[64,64]{1,0:T(8,128)(2,1)S(1)}, bf16[64,64]{1,0:T(8,128)(2,1)}, u32[]{:S(2)}) copy-start(bf16[64,64]{1,0:T(8,128)(2,1)} %constant.33.clone.order) | copy-start | bytes 24580
  120.9 3.2 %collective-permute-start.4 = (bf16[8,64,128]{2,1,0:T(8,128)(2,1)S(1)}, bf16[8,64,128]{2,1,0:T(8,128)(2,1)S(1)}, u32[]{:S(2)}, u32[]{:S(2)}) collective-permute-start(bf16[8,64,128]{2,1,0:T(8,128)(2,1)S(1)} %get-tuple-element.13.mine), channel_id=1, source_target_pairs={{0,1},{1,0},{2,3},{3,2},{4,5},{5,4},{6,7},{7,6},{8,9},{9,8},{10,11... | collective-permute-start | bytes 393224 | tf_op jit(solution)/shard_map/ppermute | solution.py:20

commit v2 on v1

--- a/solution.py
+++ b/solution.py
@@ -40,43 +40,45 @@
     return jnp.asarray(order, jnp.bfloat16)
 
 
-def pick_kernel(lists, feats, out0, out1, out2, out3, sems):
-    copies = []
+def pick_kernel(lists, feats, shell, out0, out1, out2, out3, wide):
+    @pl.loop(0, feats.shape[0])
+    def _(g):
+        shell[g, :64] = feats[g, :64]
+        shell[g, 64:128] = feats[g, 448:]
+        wide[...] = feats[g].astype(jnp.float32)
+        for a in range(1, 7):
+            start = 128 + (a - 1) * 32
+            lines = [
+                wide[a * 64 : a * 64 + 8],
+                wide[a * 64 + 56 : a * 64 + 64],
+                wide[pl.ds(a * 64, 8, stride=8)],
+                wide[pl.ds(a * 64 + 7, 8, stride=8)],
+            ]
+            shell[g, start : start + 32] = jnp.concatenate(lines).astype(jnp.bfloat16)
+
     for i, out in enumerate((out0, out1, out2, out3)):
         for slot in range(out.shape[0]):
-            copies.append(
-                pltpu.make_async_copy(
-                    feats.at[lists[i, slot]], out.at[slot], sems.at[i * out.shape[0] + slot]
-                )
-            )
-    for copy in copies:
-        copy.start()
-    for copy in copies:
-        copy.wait()
-
-
-def fill_columns(g, ids, ext, cols):
+            out[slot] = shell[lists[i, slot]]
+
+
+def fill_columns(g, ids, own, ext, cols):
     z = lax.broadcasted_iota(jnp.int32, (8, 8, 128), 1)
 
-    def band(number, plane, oy):
-        low, size = {-1: (48, 16), 0: (0, 64), 1: (0, 16)}[oy]
-        rows = ext[ids[g, number], pl.ds(plane * 64 + low, size), :].astype(jnp.float32)
-        rows = rows.reshape(size // 8, 8, 128)
-        return {-1: rows[1:], 0: rows, 1: rows[:1]}[oy]
-
-    def plane_of(place, ox, plane):
-        bands = []
-        for oy in (-1, 0, 1):
-            first = 9 * (ox + 1) + 3 * (oy + 1)
-            low, mid, high = (band(first + i, plane, oy) for i in range(3))
-            mask = z[: mid.shape[0]]
-            bands.append(
-                (
-                    pltpu.roll(jnp.where(mask == 7, low, mid), 1, 1),
-                    mid,
-                    pltpu.roll(jnp.where(mask == 0, high, mid), 7, 1),
-                )
-            )
+    def rows_of(number, start, size):
+        return ext[ids[g, number], start : start + size].astype(jnp.float32)
+
+    def spread(line):
+        return jnp.broadcast_to(line[:, None, :], (8, 8, 128))
+
+    def shifts(low, mid, high):
+        mask = z[: mid.shape[0]]
+        return (
+            pltpu.roll(jnp.where(mask == 7, low, mid), 1, 1),
+            mid,
+            pltpu.roll(jnp.where(mask == 0, high, mid), 7, 1),
+        )
+
+    def store(place, bands):
         for kz in range(3):
             whole = jnp.concatenate([bands[0][kz], bands[1][kz], bands[2][kz]], axis=0)
             for ky in range(3):
@@ -85,14 +87,49 @@
                     whole[ky : ky + 8].reshape(64, 128).astype(jnp.bfloat16)
                 )
 
-    plane_of(0, -1, 7)
-    for plane in range(8):
-        plane_of(plane + 1, 0, plane)
-    plane_of(9, 1, 0)
+    def end_plane(place, ox, start):
+        bands = []
+        for oy in (-1, 0, 1):
+            first = 9 * (ox + 1) + 3 * (oy + 1)
+            low, size = {-1: (48, 16), 0: (0, 64), 1: (0, 16)}[oy]
+            parts = []
+            for i in range(3):
+                part = rows_of(first + i, start + low, size).reshape(size // 8, 8, 128)
+                parts.append({-1: part[1:], 0: part, 1: part[:1]}[oy])
+            bands.append(shifts(*parts))
+        store(place, bands)
+
+    def inner_plane(a):
+        def line(number, which):
+            if a in (0, 7):
+                start = 0 if a == 0 else 64
+                if which < 2:
+                    return rows_of(number, start + 48 * which, 16)[8 * which : 8 * which + 8]
+                return rows_of(number, start, 64).reshape(8, 8, 128)
+            rows = rows_of(number, 128 + (a - 1) * 32 + 16 * (which // 2), 16)
+            return rows[8 * (which % 2) : 8 * (which % 2) + 8]
+
+        mid = own[g, a * 64 : (a + 1) * 64].astype(jnp.float32).reshape(8, 8, 128)
+        sides = [line(12, 3), line(14, 2)]
+        if a not in (0, 7):
+            sides = [spread(side) for side in sides]
+        store(
+            a + 1,
+            [
+                shifts(*(line(9 + i, 1)[None] for i in range(3))),
+                shifts(sides[0], mid, sides[1]),
+                shifts(*(line(15 + i, 0)[None] for i in range(3))),
+            ],
+        )
+
+    end_plane(0, -1, 64)
+    for a in range(8):
+        inner_plane(a)
+    end_plane(9, 1, 0)
 
 
 def conv_kernel(
-    ids, feats, from0, from1, from2, from3, weight, gain, shift, reduce, order,
+    ids, own, feats, from0, from1, from2, from3, weight, gain, shift, reduce, order,
     fine, octant, ext, cols, grouped, sems,
 ):
     g = pl.program_id(0)
@@ -113,7 +150,7 @@
         for copy in copies:
             copy.wait()
 
-    fill_columns(g, ids, ext, cols)
+    fill_columns(g, ids, own, ext, cols)
     total = None
     for kx in range(3):
         term = jnp.dot(
@@ -170,12 +207,15 @@
     vmem = pl.BlockSpec(memory_space=pltpu.VMEM)
     smem = pl.BlockSpec(memory_space=pltpu.SMEM)
     hbm = pl.BlockSpec(memory_space=pl.ANY)
-    outgoing = pl.pallas_call(
+    rows = 320
+    shell, *outgoing = pl.pallas_call(
         pick_kernel,
-        in_specs=[smem, hbm],
-        out_specs=[hbm] * 4,
-        out_shape=[jax.ShapeDtypeStruct((slots, 512, channels), jnp.bfloat16)] * 4,
-        scratch_shapes=[pltpu.SemaphoreType.DMA((4 * slots,))],
+        in_specs=[smem, vmem],
+        out_specs=[vmem] * 5,
+        out_shape=[jax.ShapeDtypeStruct((blocks, rows, channels), jnp.bfloat16)]
+        + [jax.ShapeDtypeStruct((slots, rows, channels), jnp.bfloat16)] * 4,
+        scratch_shapes=[pltpu.VMEM((512, channels), jnp.float32)],
+        compiler_params=pltpu.CompilerParams(vmem_limit_bytes=16 * 1024 * 1024),
     )(send_lists[0], features)
     received = [shifted(part, "cell", d) for part, d in zip(outgoing, OFFSETS)]
     self_id = jnp.arange(blocks, dtype=jnp.int32)[:, None]
@@ -185,13 +225,13 @@
         grid_spec=pltpu.PrefetchScalarGridSpec(
             num_scalar_prefetch=1,
             grid=(blocks,),
-            in_specs=[hbm] * 5 + [vmem] * 5,
+            in_specs=[vmem] + [hbm] * 5 + [vmem] * 5,
             out_specs=[
                 pl.BlockSpec((1, 512, channels), lambda g, ids: (g, 0, 0)),
                 pl.BlockSpec((1, 64, channels), lambda g, ids: (g, 0, 0)),
             ],
             scratch_shapes=[
-                pltpu.VMEM((blocks + 4 * slots + 1, 512, channels), jnp.bfloat16),
+                pltpu.VMEM((blocks + 4 * slots + 1, rows, channels), jnp.bfloat16),
                 pltpu.VMEM((10, 64, 9 * channels), jnp.bfloat16),
                 pltpu.VMEM((64, 8 * channels), jnp.bfloat16),
                 pltpu.SemaphoreType.DMA((5,)),
@@ -203,7 +243,7 @@
         ],
         compiler_params=pltpu.CompilerParams(vmem_limit_bytes=40 * 1024 * 1024),
     )(
-        ids, features, *received, conv_weight, norm_gain[None], norm_shift[None],
+        ids, features, shell, *received, conv_weight, norm_gain[None], norm_shift[None],
         reduce_weight_matrix, octant_order(),
     )
     partner_octants = swapped(octants, "cell")

time: 126 us -> 52.4 us (0.42)
  Pallas kernels: 80.7 us -> 17.4 us
  waiting for transfers between devices: 26.2 us -> 14.6 us
  local copies, waits for them, and re-layouts: 3.56 us -> 5.46 us
    pallas_call x1, Pallas kernels: 65.6 us -> 1.78 us  [per_device(): pl.pallas_call(pick_kernel, in_specs=[smem, vmem], out_specs=[vmem] * 5,...]
    ppermute x4, waiting for transfers between devices: 25.5 us -> 13.9 us  [shifted(): return lax.ppermute(block, axis, route)]
    unnamed x18 -> x22, local copies, waits for them, and re-layouts: 3.41 us -> 5.31 us
  transfers between devices with their start and end apart: 5 -> 5, of which waited for: 4 -> 3; matrix products, arithmetic and copies ran while one was open for 0% -> 1% of each run, Pallas kernels for 0% -> 0%
where the time goes in v2:
time: 52.4 us; the launch traced here: 51.6 us
  Pallas kernels  17.4 us (33%)
  waiting for transfers between devices  14.6 us (28%)
  starting transfers between devices  13 us (25%)
  local copies, waits for them, and re-layouts  5.46 us (10%)
  between operations  0.74 us (1%)
    pallas_call x1, Pallas kernels, per_device(): pl.pallas_call(conv_kernel, grid_spec=pltpu.PrefetchScalarGridSpec(num_sc...  14.2 us
    ppermute x4, waiting for transfers between devices, shifted(): return lax.ppermute(block, axis, route)  13.9 us
    ppermute x4, starting transfers between devices, shifted(): return lax.ppermute(block, axis, route)  11.8 us
    unnamed x22, local copies, waits for them, and re-layouts  5.31 us
    pallas_call x1, Pallas kernels, per_device(): pl.pallas_call(pick_kernel, in_specs=[smem, vmem], out_specs=[vmem] * 5,...  1.78 us
    pallas_call x1, Pallas kernels, per_device(): pl.pallas_call(place_kernel, in_specs=[smem, vmem, vmem, vmem], out_specs...  1.5 us
    ppermute x1, starting transfers between devices, swapped(): return lax.ppermute(block, axis, [(i, i ^ 1) for i in range(count)])  1.19 us
  transfers between devices with their start and end apart: 5, of which 3 were waited for; matrix products, arithmetic and copies ran while one was open for 1% of the time, Pallas kernels for 0%

profile of v2, /device:TPU:11, one launch (start us, length us, event | category | flops | bytes accessed | tf_op | source)
XLA Modules:
  0.0 51.6 jit_solution(5012359511825033634)
XLA Ops:
  0.6 1.2 %copy-done = bf16[8,512,128]{2,1,0:T(8,128)(2,1)S(1)} copy-done((bf16[8,512,128]{2,1,0:T(8,128)(2,1)S(1)}, bf16[8,512,128]{2,1,0:T(8,128)(2,1)}, u32[]{:S(2)}) %copy-start) | copy-done | bytes 1048600
  1.9 0.7 %copy-done.6 = s32[1,4,4]{2,1,0:T(4,128)S(1)} copy-done((s32[1,4,4]{2,1,0:T(4,128)S(1)}, s32[1,4,4]{2,1,0:T(4,128)}, u32[]{:S(2)}) %copy-start.6) | copy-done | bytes 88
  2.5 1.8 %shard_map.113 = (bf16[8,320,128]{2,1,0:T(8,128)(2,1)S(1)}, bf16[4,320,128]{2,1,0:T(8,128)(2,1)}, bf16[4,320,128]{2,1,0:T(8,128)(2,1)}, bf16[4,320,128]{2,1,0:T(8,128)(2,1)}, bf16[4,320,128]{2,1,0:T(8,128)(2,1)S(1)}) custom-call(s32[4,4]{1,0:T(4,128)S(1)} %bitcast.3, bf16[8,512,128]{2,1,0:T(8,128)(2,1)S(1)} %copy-done), custom_call_target="tpu_custom_call" | custom-call | tf_op jit(solution)/shard_map/pallas_call | solution.py:211
  4.3 3.7 %collective-permute-start = (bf16[4,320,128]{2,1,0:T(8,128)(2,1)}, bf16[4,320,128]{2,1,0:T(8,128)(2,1)S(1)}, u32[]{:S(2)}, u32[]{:S(2)}) collective-permute-start(bf16[4,320,128]{2,1,0:T(8,128)(2,1)} %get-tuple-element.10), channel_id=1, source_target_pairs={{0,1},{1,2},{2,3},{3,4},{4,5},{5,6},{6,7},{7,8},{8,9},{9,10},{10,1... | collective-permute-start | bytes 983048 | tf_op jit(solution)/shard_map/ppermute | solution.py:15
  8.0 1.9 %collective-permute-start.1 = (bf16[4,320,128]{2,1,0:T(8,128)(2,1)}, bf16[4,320,128]{2,1,0:T(8,128)(2,1)S(1)}, u32[]{:S(2)}, u32[]{:S(2)}) collective-permute-start(bf16[4,320,128]{2,1,0:T(8,128)(2,1)} %get-tuple-element.11), channel_id=1, source_target_pairs={{1,0},{2,1},{3,2},{4,3},{5,4},{6,5},{7,6},{8,7},{9,8},{10,9},{11,1... | collective-permute-start | bytes 983048 | tf_op jit(solution)/shard_map/ppermute | solution.py:15
  9.9 3.1 %collective-permute-start.2 = (bf16[4,320,128]{2,1,0:T(8,128)(2,1)}, bf16[4,320,128]{2,1,0:T(8,128)(2,1)S(1)}, u32[]{:S(2)}, u32[]{:S(2)}) collective-permute-start(bf16[4,320,128]{2,1,0:T(8,128)(2,1)} %get-tuple-element.12), channel_id=1, source_target_pairs={{0,2},{1,3},{2,4},{3,5},{4,6},{5,7},{6,8},{7,9},{8,10},{9,11},{10,... | collective-permute-start | bytes 983048 | tf_op jit(solution)/shard_map/ppermute | solution.py:15
  13.1 3.0 %collective-permute-start.3 = (bf16[4,320,128]{2,1,0:T(8,128)(2,1)S(1)}, bf16[4,320,128]{2,1,0:T(8,128)(2,1)S(1)}, u32[]{:S(2)}, u32[]{:S(2)}) collective-permute-start(bf16[4,320,128]{2,1,0:T(8,128)(2,1)S(1)} %get-tuple-element.13), channel_id=1, source_target_pairs={{2,0},{3,1},{4,2},{5,3},{6,4},{7,5},{8,6},{9,7},{10,8},{11,9},{12,... | collective-permute-start | bytes 983048 | tf_op jit(solution)/shard_map/ppermute | solution.py:15
  16.2 0.0 copy-start.4
  16.2 0.6 %copy-done.10 = s32[128]{0:T(128)S(1)} copy-done((s32[128]{0:T(128)S(1)}, s32[128]{0:T(128)}, u32[]{:S(2)}) %copy-start.10) | copy-done | bytes 536
  16.8 0.1 fusion.1
  16.9 0.1 fusion
  17.0 0.1 pad_add_fusion.ids
  17.0 9.1 %collective-permute-done.1.from1 = bf16[4,320,128]{2,1,0:T(8,128)(2,1)S(1)} collective-permute-done((bf16[4,320,128]{2,1,0:T(8,128)(2,1)}, bf16[4,320,128]{2,1,0:T(8,128)(2,1)S(1)}, u32[]{:S(2)}, u32[]{:S(2)}) %collective-permute-start.1) | collective-permute-done | bytes 327712 | tf_op jit(solution)/shard_map/ppermute | solution.py:15
  26.1 4.8 %collective-permute-done.2.from2 = bf16[4,320,128]{2,1,0:T(8,128)(2,1)S(1)} collective-permute-done((bf16[4,320,128]{2,1,0:T(8,128)(2,1)}, bf16[4,320,128]{2,1,0:T(8,128)(2,1)S(1)}, u32[]{:S(2)}, u32[]{:S(2)}) %collective-permute-start.2) | collective-permute-done | bytes 327712 | tf_op jit(solution)/shard_map/ppermute | solution.py:15
  30.9 0.6 %copy-done.7 = f32[128]{0:T(128)S(1)} copy-done((f32[128]{0:T(128)S(1)}, f32[128]{0:T(128)}, u32[]{:S(2)}) %copy-start.7) | copy-done | bytes 536
  31.6 0.0 copy-done.8
  31.6 1.2 %copy-done.2 = bf16[3456,128]{1,0:T(8,128)(2,1)S(1)} copy-done((bf16[3456,128]{1,0:T(8,128)(2,1)S(1)}, bf16[3456,128]{1,0:T(8,128)(2,1)}, u32[]{:S(2)}) %copy-start.2) | copy-done | bytes 884760
  32.8 0.9 %copy-done.3 = bf16[1024,128]{1,0:T(8,128)(2,1)S(1)} copy-done((bf16[1024,128]{1,0:T(8,128)(2,1)S(1)}, bf16[1024,128]{1,0:T(8,128)(2,1)}, u32[]{:S(2)}) %copy-start.3) | copy-done | bytes 262168
  33.7 14.2 %shard_map.114 = (bf16[8,512,128]{2,1,0:T(8,128)(2,1)}, bf16[8,64,128]{2,1,0:T(8,128)(2,1)S(1)}) custom-call(s32[8,27]{1,0:T(8,128)S(1)} %pad_add_fusion.ids, bf16[8,512,128]{2,1,0:T(8,128)(2,1)S(1)} %copy-done.1, bf16[8,320,128]{2,1,0:T(8,128)(2,1)S(1)} %get-tuple-element.9.feats, bf16[4,320,128]{2,1,0:T(8,128)(2,1)S(1)} %collective-permute-done.from0, ...), custom_call_target="tpu_custom_call" | custom-call | tf_op jit(solution)/shard_map/pallas_call | solution.py:223
  47.9 1.2 %collective-permute-start.4 = (bf16[8,64,128]{2,1,0:T(8,128)(2,1)S(1)}, bf16[8,64,128]{2,1,0:T(8,128)(2,1)S(1)}, u32[]{:S(2)}, u32[]{:S(2)}) collective-permute-start(bf16[8,64,128]{2,1,0:T(8,128)(2,1)S(1)} %get-tuple-element.15.mine), channel_id=1, source_target_pairs={{0,1},{1,0},{2,3},{3,2},{4,5},{5,4},{6,7},{7,6},{8,9},{9,8},{10,11... | collective-permute-start | bytes 393224 | tf_op jit(solution)/shard_map/ppermute | solution.py:20
  49.1 0.1 pad_add_fusion.1
  49.1 0.2 select_reduce_fusion.source
  49.3 0.7 %collective-permute-done.4.other = bf16[8,64,128]{2,1,0:T(8,128)(2,1)S(1)} collective-permute-done((bf16[8,64,128]{2,1,0:T(8,128)(2,1)S(1)}, bf16[8,64,128]{2,1,0:T(8,128)(2,1)S(1)}, u32[]{:S(2)}, u32[]{:S(2)}) %collective-permute-start.4) | collective-permute-done | bytes 131104 | tf_op jit(solution)/shard_map/ppermute | solution.py:20
  50.1 1.5 %shard_map.115 = bf16[2,512,128]{2,1,0:T(8,128)(2,1)} custom-call(s32[16]{0:T(128)S(1)} %select_reduce_fusion.source, bf16[8,64,128]{2,1,0:T(8,128)(2,1)S(1)} %get-tuple-element.15.mine, bf16[8,64,128]{2,1,0:T(8,128)(2,1)S(1)} %collective-permute-done.4.other, bf16[64,64]{1,0:T(8,128)(2,1)S(1)} %copy-done.5), custom_call_target="tpu_custom_call" | custom-call | tf_op jit(solution)/shard_map/pallas_call | solution.py:261
  (17 shorter events, 0.0 us)
Async XLA Ops:
  0.6 1.2 %copy-start = (bf16[8,512,128]{2,1,0:T(8,128)(2,1)S(1)}, bf16[8,512,128]{2,1,0:T(8,128)(2,1)}, u32[]{:S(2)}) copy-start(bf16[8,512,128]{2,1,0:T(8,128)(2,1)} %own.1) | copy-start | bytes 3145732
  1.9 0.7 %copy-start.6 = (s32[1,4,4]{2,1,0:T(4,128)S(1)}, s32[1,4,4]{2,1,0:T(4,128)}, u32[]{:S(2)}) copy-start(s32[1,4,4]{2,1,0:T(4,128)} %param.12) | copy-start | bytes 196
  2.5 28.4 %copy-start.1 = (bf16[8,512,128]{2,1,0:T(8,128)(2,1)S(1)}, bf16[8,512,128]{2,1,0:T(8,128)(2,1)}, u32[]{:S(2)}) copy-start(bf16[8,512,128]{2,1,0:T(8,128)(2,1)} %own.1) | copy-start | bytes 3145732
  4.3 12.7 %collective-permute-start = (bf16[4,320,128]{2,1,0:T(8,128)(2,1)}, bf16[4,320,128]{2,1,0:T(8,128)(2,1)S(1)}, u32[]{:S(2)}, u32[]{:S(2)}) collective-permute-start(bf16[4,320,128]{2,1,0:T(8,128)(2,1)} %get-tuple-element.10), channel_id=1, source_target_pairs={{0,1},{1,2},{2,3},{3,4},{4,5},{5,6},{6,7},{7,8},{8,9},{9,10},{10,1... | collective-permute-start | bytes 983048 | tf_op jit(solution)/shard_map/ppermute | solution.py:15
  8.0 18.1 %collective-permute-start.1 = (bf16[4,320,128]{2,1,0:T(8,128)(2,1)}, bf16[4,320,128]{2,1,0:T(8,128)(2,1)S(1)}, u32[]{:S(2)}, u32[]{:S(2)}) collective-permute-start(bf16[4,320,128]{2,1,0:T(8,128)(2,1)} %get-tuple-element.11), channel_id=1, source_target_pairs={{1,0},{2,1},{3,2},{4,3},{5,4},{6,5},{7,6},{8,7},{9,8},{10,9},{11,1... | collective-permute-start | bytes 983048 | tf_op jit(solution)/shard_map/ppermute | solution.py:15
  9.9 21.0 %collective-permute-start.2 = (bf16[4,320,128]{2,1,0:T(8,128)(2,1)}, bf16[4,320,128]{2,1,0:T(8,128)(2,1)S(1)}, u32[]{:S(2)}, u32[]{:S(2)}) collective-permute-start(bf16[4,320,128]{2,1,0:T(8,128)(2,1)} %get-tuple-element.12), channel_id=1, source_target_pairs={{0,2},{1,3},{2,4},{3,5},{4,6},{5,7},{6,8},{7,9},{8,10},{9,11},{10,... | collective-permute-start | bytes 983048 | tf_op jit(solution)/shard_map/ppermute | solution.py:15
  13.1 17.8 %collective-permute-start.3 = (bf16[4,320,128]{2,1,0:T(8,128)(2,1)S(1)}, bf16[4,320,128]{2,1,0:T(8,128)(2,1)S(1)}, u32[]{:S(2)}, u32[]{:S(2)}) collective-permute-start(bf16[4,320,128]{2,1,0:T(8,128)(2,1)S(1)} %get-tuple-element.13), channel_id=1, source_target_pairs={{2,0},{3,1},{4,2},{5,3},{6,4},{7,5},{8,6},{9,7},{10,8},{11,9},{12,... | collective-permute-start | bytes 983048 | tf_op jit(solution)/shard_map/ppermute | solution.py:15
  16.2 0.7 %copy-start.10 = (s32[128]{0:T(128)S(1)}, s32[128]{0:T(128)}, u32[]{:S(2)}) copy-start(s32[128]{0:T(128)} %param.13) | copy-start | bytes 1540
  16.2 0.7 %copy-start.9 = (s32[8,26]{1,0:T(8,128)S(1)}, s32[8,26]{1,0:T(8,128)}, u32[]{:S(2)}) copy-start(s32[8,26]{1,0:T(8,128)} %param.11) | copy-start | bytes 2500
  16.2 14.7 %copy-start.4 = (bf16[128,128]{1,0:T(8,128)(2,1)S(1)}, bf16[128,128]{1,0:T(8,128)(2,1)}, u32[]{:S(2)}) copy-start(bf16[128,128]{1,0:T(8,128)(2,1)} %constant.32.clone.order) | copy-start | bytes 98308
  30.9 0.7 %copy-start.7 = (f32[128]{0:T(128)S(1)}, f32[128]{0:T(128)}, u32[]{:S(2)}) copy-start(f32[128]{0:T(128)} %param.15) | copy-start | bytes 1540
  30.9 0.7 %copy-start.8 = (f32[128]{0:T(128)S(1)}, f32[128]{0:T(128)}, u32[]{:S(2)}) copy-start(f32[128]{0:T(128)} %param.16) | copy-start | bytes 1540
  31.6 1.2 %copy-start.2 = (bf16[3456,128]{1,0:T(8,128)(2,1)S(1)}, bf16[3456,128]{1,0:T(8,128)(2,1)}, u32[]{:S(2)}) copy-start(bf16[3456,128]{1,0:T(8,128)(2,1)} %weight.1) | copy-start | bytes 2654212
  32.8 0.9 %copy-start.3 = (bf16[1024,128]{1,0:T(8,128)(2,1)S(1)}, bf16[1024,128]{1,0:T(8,128)(2,1)}, u32[]{:S(2)}) copy-start(bf16[1024,128]{1,0:T(8,128)(2,1)} %reduce.1) | copy-start | bytes 786436
  33.7 16.4 %copy-start.5 = (bf16[64,64]{1,0:T(8,128)(2,1)S(1)}, bf16[64,64]{1,0:T(8,128)(2,1)}, u32[]{:S(2)}) copy-start(bf16[64,64]{1,0:T(8,128)(2,1)} %constant.33.clone.order) | copy-start | bytes 24580
  47.9 2.2 %collective-permute-start.4 = (bf16[8,64,128]{2,1,0:T(8,128)(2,1)S(1)}, bf16[8,64,128]{2,1,0:T(8,128)(2,1)S(1)}, u32[]{:S(2)}, u32[]{:S(2)}) collective-permute-start(bf16[8,64,128]{2,1,0:T(8,128)(2,1)S(1)} %get-tuple-element.15.mine), channel_id=1, source_target_pairs={{0,1},{1,0},{2,3},{3,2},{4,5},{5,4},{6,7},{7,6},{8,9},{9,8},{10,11... | collective-permute-start | bytes 393224 | tf_op jit(solution)/shard_map/ppermute | solution.py:20

commit v3 on v2

--- a/solution.py
+++ b/solution.py
@@ -7,12 +7,6 @@
 from jax.sharding import PartitionSpec as P
 
 OFFSETS = (1, -1, 2, -2)
-
-
-def shifted(block, axis, distance):
-    devices = range(lax.axis_size(axis))
-    route = [(i - distance, i) for i in devices if i - distance in devices]
-    return lax.ppermute(block, axis, route)
 
 
 def swapped(block, axis):
@@ -40,7 +34,23 @@
     return jnp.asarray(order, jnp.bfloat16)
 
 
-def pick_kernel(lists, feats, shell, out0, out1, out2, out3, wide):
+def exchange_kernel(
+    lists, feats, shell, in0, in1, in2, in3, wide, out0, out1, out2, out3, sent, landed
+):
+    me, count = lax.axis_index("cell"), lax.axis_size("cell")
+    barrier = pltpu.get_barrier_semaphore()
+
+    def there(device):
+        return (device >= 0) & (device < count)
+
+    for d in OFFSETS:
+
+        @pl.when(there(me + d))
+        def _(d=d):
+            pl.semaphore_signal(
+                barrier, inc=1, device_id={"cell": me + d}, device_id_type=pl.DeviceIdType.MESH
+            )
+
     @pl.loop(0, feats.shape[0])
     def _(g):
         shell[g, :64] = feats[g, :64]
@@ -59,6 +69,36 @@
     for i, out in enumerate((out0, out1, out2, out3)):
         for slot in range(out.shape[0]):
             out[slot] = shell[lists[i, slot]]
+
+    pl.semaphore_wait(barrier, sum(there(me + d).astype(jnp.int32) for d in OFFSETS))
+
+    copies = []
+    for i, (d, out, into) in enumerate(
+        zip(OFFSETS, (out0, out1, out2, out3), (in0, in1, in2, in3))
+    ):
+        copy = pltpu.make_async_remote_copy(
+            src_ref=out,
+            dst_ref=into,
+            send_sem=sent.at[i],
+            recv_sem=landed.at[i],
+            device_id={"cell": me + d},
+            device_id_type=pl.DeviceIdType.MESH,
+        )
+        copies.append(copy)
+        pl.when(there(me + d))(copy.start)
+    for d, into, copy in zip(OFFSETS, (in0, in1, in2, in3), copies):
+
+        @pl.when(there(me - d))
+        def _(copy=copy):
+            copy.wait_recv()
+
+        @pl.when(jnp.logical_not(there(me - d)))
+        def _(into=into):
+            into[...] = jnp.zeros_like(into)
+
+        @pl.when(there(me + d))
+        def _(copy=copy):
+            copy.wait_send()
 
 
 def fill_columns(g, ids, own, ext, cols):
@@ -208,16 +248,19 @@
     smem = pl.BlockSpec(memory_space=pltpu.SMEM)
     hbm = pl.BlockSpec(memory_space=pl.ANY)
     rows = 320
-    shell, *outgoing = pl.pallas_call(
-        pick_kernel,
+    shell, *received = pl.pallas_call(
+        exchange_kernel,
         in_specs=[smem, vmem],
         out_specs=[vmem] * 5,
         out_shape=[jax.ShapeDtypeStruct((blocks, rows, channels), jnp.bfloat16)]
         + [jax.ShapeDtypeStruct((slots, rows, channels), jnp.bfloat16)] * 4,
-        scratch_shapes=[pltpu.VMEM((512, channels), jnp.float32)],
-        compiler_params=pltpu.CompilerParams(vmem_limit_bytes=16 * 1024 * 1024),
+        scratch_shapes=[pltpu.VMEM((512, channels), jnp.float32)]
+        + [pltpu.VMEM((slots, rows, channels), jnp.bfloat16)] * 4
+        + [pltpu.SemaphoreType.DMA((4,)), pltpu.SemaphoreType.DMA((4,))],
+        compiler_params=pltpu.CompilerParams(
+            vmem_limit_bytes=24 * 1024 * 1024, collective_id=0, has_side_effects=True
+        ),
     )(send_lists[0], features)
-    received = [shifted(part, "cell", d) for part, d in zip(outgoing, OFFSETS)]
     self_id = jnp.arange(blocks, dtype=jnp.int32)[:, None]
     ids = jnp.concatenate([neighbour_table[:, :13], self_id, neighbour_table[:, 13:]], axis=1)
     fine, octants = pl.pallas_call(

time: 52.4 us -> 49 us (0.935)
  Pallas kernels: 17.4 us -> 39.7 us
  waiting for transfers between devices: 14.6 us -> 0.01 us
  starting transfers between devices: 13 us -> 2.32 us
    pallas_call x1, Pallas kernels: 1.78 us -> 24 us  [per_device(): pl.pallas_call(exchange_kernel, in_specs=[smem, vmem], out_specs=[vmem] *...]
    ppermute x4 -> x0, waiting for transfers between devices: 13.9 us -> none  [shifted(): return lax.ppermute(block, axis, route)]
    ppermute x4 -> x0, starting transfers between devices: 11.8 us -> none  [shifted(): return lax.ppermute(block, axis, route)]
    ppermute x1, starting transfers between devices: 1.19 us -> 2.32 us  [swapped(): return lax.ppermute(block, axis, [(i, i ^ 1) for i in range(count)])]
    slice x1, local copies, waits for them, and re-layouts: 0.07 us -> 0.83 us  [per_device(): neighbour_table[:, :13]]
    ppermute x1, waiting for transfers between devices: 0.72 us -> 0.01 us  [swapped(): return lax.ppermute(block, axis, [(i, i ^ 1) for i in range(count)])]
    unnamed x22 -> x20, local copies, waits for them, and re-layouts: 5.31 us -> 4.69 us
  transfers between devices with their start and end apart: 5 -> 1, of which waited for: 3 -> 0; matrix products, arithmetic and copies ran while one was open for 1% -> 1% of each run, Pallas kernels for 0% -> 0%
where the time goes in v3:
time: 49 us; the launch traced here: 48.7 us
  Pallas kernels  39.7 us (81%)
  local copies, waits for them, and re-layouts  5.61 us (11%)
  starting transfers between devices  2.32 us (5%)
  between operations  0.69 us (1%)
    pallas_call x1, Pallas kernels, per_device(): pl.pallas_call(exchange_kernel, in_specs=[smem, vmem], out_specs=[vmem] *...  24 us
    pallas_call x1, Pallas kernels, per_device(): pl.pallas_call(conv_kernel, grid_spec=pltpu.PrefetchScalarGridSpec(num_sc...  14.2 us
    unnamed x20, local copies, waits for them, and re-layouts  4.69 us
    ppermute x1, starting transfers between devices, swapped(): return lax.ppermute(block, axis, [(i, i ^ 1) for i in range(count)])  2.32 us
    pallas_call x1, Pallas kernels, per_device(): pl.pallas_call(place_kernel, in_specs=[smem, vmem, vmem, vmem], out_specs...  1.5 us
  transfers between devices with their start and end apart: 1, of which 0 were waited for; matrix products, arithmetic and copies ran while one was open for 1% of the time, Pallas kernels for 0%

profile of v3, /device:TPU:11, one launch (start us, length us, event | category | flops | bytes accessed | tf_op | source)
XLA Modules:
  0.0 48.7 jit_solution(2063338583675891589)
XLA Ops:
  0.6 0.0 copy-start.6
  0.6 0.8 %fusion = (s32[8,13]{1,0:T(8,128)S(1)}, s32[8,13]{1,0:T(8,128)S(1)}) fusion(s32[8,26]{1,0:T(8,128)} %param.11), kind=kLoop, calls=%fused_computation.4 | loop fusion | bytes 1664 | tf_op jit(solution)/shard_map/slice | solution.py:265
  1.5 0.0 copy-done.6
  1.5 0.0 copy-start
  1.5 1.2 %copy-done = bf16[8,512,128]{2,1,0:T(8,128)(2,1)S(1)} copy-done((bf16[8,512,128]{2,1,0:T(8,128)(2,1)S(1)}, bf16[8,512,128]{2,1,0:T(8,128)(2,1)}, u32[]{:S(2)}) %copy-start) | copy-done | bytes 1048600
  2.7 0.0 copy-start.1
  2.7 24.0 %shard_map.113 = (bf16[8,320,128]{2,1,0:T(8,128)(2,1)S(1)}, bf16[4,320,128]{2,1,0:T(8,128)(2,1)S(1)}, bf16[4,320,128]{2,1,0:T(8,128)(2,1)S(1)}, bf16[4,320,128]{2,1,0:T(8,128)(2,1)S(1)}, bf16[4,320,128]{2,1,0:T(8,128)(2,1)S(1)}) custom-call(s32[4,4]{1,0:T(4,128)S(1)} %bitcast.3, bf16[8,512,128]{2,1,0:T(8,128)(2,1)S(1)} %copy-done), custom_call_target="tpu_custom_call" | custom-call | tf_op jit(solution)/shard_map/pallas_call | solution.py:251
  26.8 0.0 copy-start.4
  26.8 0.1 pad_add_fusion.ids
  26.9 0.0 copy-done.1
  26.9 0.7 %copy-done.4 = bf16[128,128]{1,0:T(8,128)(2,1)S(1)} copy-done((bf16[128,128]{1,0:T(8,128)(2,1)S(1)}, bf16[128,128]{1,0:T(8,128)(2,1)}, u32[]{:S(2)}) %copy-start.4) | copy-done | bytes 32792
  27.5 0.0 copy-done.7
  27.5 0.0 copy-done.8
  27.5 1.2 %copy-done.2 = bf16[3456,128]{1,0:T(8,128)(2,1)S(1)} copy-done((bf16[3456,128]{1,0:T(8,128)(2,1)S(1)}, bf16[3456,128]{1,0:T(8,128)(2,1)}, u32[]{:S(2)}) %copy-start.2) | copy-done | bytes 884760
  28.7 0.9 %copy-done.3 = bf16[1024,128]{1,0:T(8,128)(2,1)S(1)} copy-done((bf16[1024,128]{1,0:T(8,128)(2,1)S(1)}, bf16[1024,128]{1,0:T(8,128)(2,1)}, u32[]{:S(2)}) %copy-start.3) | copy-done | bytes 262168
  29.7 14.2 %shard_map.114 = (bf16[8,512,128]{2,1,0:T(8,128)(2,1)}, bf16[8,64,128]{2,1,0:T(8,128)(2,1)S(1)}) custom-call(s32[8,27]{1,0:T(8,128)S(1)} %pad_add_fusion.ids, bf16[8,512,128]{2,1,0:T(8,128)(2,1)S(1)} %copy-done.1, bf16[8,320,128]{2,1,0:T(8,128)(2,1)S(1)} %get-tuple-element.9.feats, bf16[4,320,128]{2,1,0:T(8,128)(2,1)S(1)} %get-tuple-element.10.from0, ...), custom_call_target="tpu_custom_call" | custom-call | tf_op jit(solution)/shard_map/pallas_call | solution.py:266
  43.8 2.3 %collective-permute-start = (bf16[8,64,128]{2,1,0:T(8,128)(2,1)S(1)}, bf16[8,64,128]{2,1,0:T(8,128)(2,1)S(1)}, u32[]{:S(2)}, u32[]{:S(2)}) collective-permute-start(bf16[8,64,128]{2,1,0:T(8,128)(2,1)S(1)} %get-tuple-element.15.mine), channel_id=1, source_target_pairs={{0,1},{1,0},{2,3},{3,2},{4,5},{5,4},{6,7},{7,6},{8,9},{9,8},{10,11... | collective-permute-start | bytes 393224 | tf_op jit(solution)/shard_map/ppermute | solution.py:14
  46.1 0.7 %copy-done.9 = s32[128]{0:T(128)S(1)} copy-done((s32[128]{0:T(128)S(1)}, s32[128]{0:T(128)}, u32[]{:S(2)}) %copy-start.9) | copy-done | bytes 536
  46.8 0.1 fusion.1
  46.9 0.1 pad_add_fusion.1
  47.0 0.2 select_reduce_fusion.source
  47.2 0.0 collective-permute-done.other
  47.2 0.0 copy-done.5
  47.2 1.5 %shard_map.115 = bf16[2,512,128]{2,1,0:T(8,128)(2,1)} custom-call(s32[16]{0:T(128)S(1)} %select_reduce_fusion.source, bf16[8,64,128]{2,1,0:T(8,128)(2,1)S(1)} %get-tuple-element.15.mine, bf16[8,64,128]{2,1,0:T(8,128)(2,1)S(1)} %collective-permute-done.other, bf16[64,64]{1,0:T(8,128)(2,1)S(1)} %copy-done.5), custom_call_target="tpu_custom_call" | custom-call | tf_op jit(solution)/shard_map/pallas_call | solution.py:304
  (7 shorter events, 0.0 us)
Async XLA Ops:
  0.6 0.8 %copy-start.6 = (s32[1,4,4]{2,1,0:T(4,128)S(1)}, s32[1,4,4]{2,1,0:T(4,128)}, u32[]{:S(2)}) copy-start(s32[1,4,4]{2,1,0:T(4,128)} %param.12) | copy-start | bytes 196
  1.5 1.2 %copy-start = (bf16[8,512,128]{2,1,0:T(8,128)(2,1)S(1)}, bf16[8,512,128]{2,1,0:T(8,128)(2,1)}, u32[]{:S(2)}) copy-start(bf16[8,512,128]{2,1,0:T(8,128)(2,1)} %own.1) | copy-start | bytes 3145732
  2.7 24.2 %copy-start.1 = (bf16[8,512,128]{2,1,0:T(8,128)(2,1)S(1)}, bf16[8,512,128]{2,1,0:T(8,128)(2,1)}, u32[]{:S(2)}) copy-start(bf16[8,512,128]{2,1,0:T(8,128)(2,1)} %own.1) | copy-start | bytes 3145732
  26.8 0.8 %copy-start.4 = (bf16[128,128]{1,0:T(8,128)(2,1)S(1)}, bf16[128,128]{1,0:T(8,128)(2,1)}, u32[]{:S(2)}) copy-start(bf16[128,128]{1,0:T(8,128)(2,1)} %constant.32.clone.order) | copy-start | bytes 98308
  26.9 0.7 %copy-start.7 = (f32[128]{0:T(128)S(1)}, f32[128]{0:T(128)}, u32[]{:S(2)}) copy-start(f32[128]{0:T(128)} %param.15) | copy-start | bytes 1540
  26.9 0.7 %copy-start.8 = (f32[128]{0:T(128)S(1)}, f32[128]{0:T(128)}, u32[]{:S(2)}) copy-start(f32[128]{0:T(128)} %param.16) | copy-start | bytes 1540
  27.5 1.2 %copy-start.2 = (bf16[3456,128]{1,0:T(8,128)(2,1)S(1)}, bf16[3456,128]{1,0:T(8,128)(2,1)}, u32[]{:S(2)}) copy-start(bf16[3456,128]{1,0:T(8,128)(2,1)} %weight.1) | copy-start | bytes 2654212
  28.7 0.9 %copy-start.3 = (bf16[1024,128]{1,0:T(8,128)(2,1)S(1)}, bf16[1024,128]{1,0:T(8,128)(2,1)}, u32[]{:S(2)}) copy-start(bf16[1024,128]{1,0:T(8,128)(2,1)} %reduce.1) | copy-start | bytes 786436
  43.8 3.3 %collective-permute-start = (bf16[8,64,128]{2,1,0:T(8,128)(2,1)S(1)}, bf16[8,64,128]{2,1,0:T(8,128)(2,1)S(1)}, u32[]{:S(2)}, u32[]{:S(2)}) collective-permute-start(bf16[8,64,128]{2,1,0:T(8,128)(2,1)S(1)} %get-tuple-element.15.mine), channel_id=1, source_target_pairs={{0,1},{1,0},{2,3},{3,2},{4,5},{5,4},{6,7},{7,6},{8,9},{9,8},{10,11... | collective-permute-start | bytes 393224 | tf_op jit(solution)/shard_map/ppermute | solution.py:14
  46.1 1.0 %copy-start.5 = (bf16[64,64]{1,0:T(8,128)(2,1)S(1)}, bf16[64,64]{1,0:T(8,128)(2,1)}, u32[]{:S(2)}) copy-start(bf16[64,64]{1,0:T(8,128)(2,1)} %constant.33.clone.order) | copy-start | bytes 24580
  46.1 0.7 %copy-start.9 = (s32[128]{0:T(128)S(1)}, s32[128]{0:T(128)}, u32[]{:S(2)}) copy-start(s32[128]{0:T(128)} %param.13) | copy-start | bytes 1540

commit v4 on v3

--- a/solution.py
+++ b/solution.py
@@ -105,7 +105,7 @@
     z = lax.broadcasted_iota(jnp.int32, (8, 8, 128), 1)
 
     def rows_of(number, start, size):
-        return ext[ids[g, number], start : start + size].astype(jnp.float32)
+        return ext[ids[g, number - (number > 13)], start : start + size].astype(jnp.float32)
 
     def spread(line):
         return jnp.broadcast_to(line[:, None, :], (8, 8, 128))
@@ -170,7 +170,7 @@
 
 def conv_kernel(
     ids, own, feats, from0, from1, from2, from3, weight, gain, shift, reduce, order,
-    fine, octant, ext, cols, grouped, sems,
+    fine, octant, ext, even, odd, grouped, sems,
 ):
     g = pl.program_id(0)
     blocks, slots = feats.shape[0], from0.shape[0]
@@ -190,26 +190,34 @@
         for copy in copies:
             copy.wait()
 
-    fill_columns(g, ids, own, ext, cols)
-    total = None
-    for kx in range(3):
-        term = jnp.dot(
-            cols[kx : kx + 8].reshape(512, 1152),
-            weight[kx * 1152 : (kx + 1) * 1152],
-            preferred_element_type=jnp.float32,
-        )
-        total = term if total is None else total + term
-    out = jnp.maximum(total * gain[...] + shift[...], 0.0).astype(jnp.bfloat16)
-    fine[0] = out
-    for a in range(4):
-        rows = jnp.dot(
-            order[...], out[a * 128 : (a + 1) * 128], preferred_element_type=jnp.float32
+    def finish(slot, cols):
+        total = None
+        for kx in range(3):
+            term = jnp.dot(
+                cols[kx : kx + 8].reshape(512, 1152),
+                weight[kx * 1152 : (kx + 1) * 1152],
+                preferred_element_type=jnp.float32,
+            )
+            total = term if total is None else total + term
+        out = jnp.maximum(total * gain[...] + shift[...], 0.0).astype(jnp.bfloat16)
+        fine[slot] = out
+        for a in range(4):
+            rows = jnp.dot(
+                order[...], out[a * 128 : (a + 1) * 128], preferred_element_type=jnp.float32
+            ).astype(jnp.bfloat16)
+            for p in range(8):
+                grouped[slot, a * 16 : (a + 1) * 16, p * 128 : (p + 1) * 128] = rows[
+                    p * 16 : (p + 1) * 16
+                ]
+        octant[slot] = jnp.dot(
+            grouped[slot], reduce[...], preferred_element_type=jnp.float32
         ).astype(jnp.bfloat16)
-        for p in range(8):
-            grouped[a * 16 : (a + 1) * 16, p * 128 : (p + 1) * 128] = rows[p * 16 : (p + 1) * 16]
-    octant[0] = jnp.dot(
-        grouped[...], reduce[...], preferred_element_type=jnp.float32
-    ).astype(jnp.bfloat16)
+
+    pl.when(g == 0)(lambda: fill_columns(0, ids, own, ext, even))
+    fill_columns(2 * g + 1, ids, own, ext, odd)
+    finish(0, even)
+    fill_columns(jnp.minimum(2 * g + 2, blocks - 2), ids, own, ext, even)
+    finish(1, odd)
 
 
 def place_kernel(source, mine, other, order, coarse, rows, stack):
@@ -257,26 +265,26 @@
         scratch_shapes=[pltpu.VMEM((512, channels), jnp.float32)]
         + [pltpu.VMEM((slots, rows, channels), jnp.bfloat16)] * 4
         + [pltpu.SemaphoreType.DMA((4,)), pltpu.SemaphoreType.DMA((4,))],
+        cost_estimate=pl.CostEstimate(flops=0, bytes_accessed=60_000_000, transcendentals=0),
         compiler_params=pltpu.CompilerParams(
             vmem_limit_bytes=24 * 1024 * 1024, collective_id=0, has_side_effects=True
         ),
     )(send_lists[0], features)
-    self_id = jnp.arange(blocks, dtype=jnp.int32)[:, None]
-    ids = jnp.concatenate([neighbour_table[:, :13], self_id, neighbour_table[:, 13:]], axis=1)
     fine, octants = pl.pallas_call(
         conv_kernel,
         grid_spec=pltpu.PrefetchScalarGridSpec(
             num_scalar_prefetch=1,
-            grid=(blocks,),
+            grid=(blocks // 2,),
             in_specs=[vmem] + [hbm] * 5 + [vmem] * 5,
             out_specs=[
-                pl.BlockSpec((1, 512, channels), lambda g, ids: (g, 0, 0)),
-                pl.BlockSpec((1, 64, channels), lambda g, ids: (g, 0, 0)),
+                pl.BlockSpec((2, 512, channels), lambda g, ids: (g, 0, 0)),
+                pl.BlockSpec((2, 64, channels), lambda g, ids: (g, 0, 0)),
             ],
             scratch_shapes=[
                 pltpu.VMEM((blocks + 4 * slots + 1, rows, channels), jnp.bfloat16),
                 pltpu.VMEM((10, 64, 9 * channels), jnp.bfloat16),
-                pltpu.VMEM((64, 8 * channels), jnp.bfloat16),
+                pltpu.VMEM((10, 64, 9 * channels), jnp.bfloat16),
+                pltpu.VMEM((2, 64, 8 * channels), jnp.bfloat16),
                 pltpu.SemaphoreType.DMA((5,)),
             ],
         ),
@@ -284,9 +292,14 @@
             jax.ShapeDtypeStruct((blocks, 512, channels), jnp.bfloat16),
             jax.ShapeDtypeStruct((blocks, 64, channels), jnp.bfloat16),
         ],
+        cost_estimate=pl.CostEstimate(
+            flops=2 * blocks * 512 * conv_weight.shape[0] * channels,
+            bytes_accessed=30_000_000,
+            transcendentals=0,
+        ),
         compiler_params=pltpu.CompilerParams(vmem_limit_bytes=40 * 1024 * 1024),
     )(
-        ids, features, shell, *received, conv_weight, norm_gain[None], norm_shift[None],
+        neighbour_table, features, shell, *received, conv_weight, norm_gain[None], norm_shift[None],
         reduce_weight_matrix, octant_order(),
     )
     partner_octants = swapped(octants, "cell")

time: 49 us -> 50.2 us (1.024)
  Pallas kernels: 39.7 us -> 40.4 us
  local copies, waits for them, and re-layouts: 5.61 us -> 6.19 us
    unnamed x20 -> x22, local copies, waits for them, and re-layouts: 4.69 us -> 6.11 us
    slice x1 -> x0, local copies, waits for them, and re-layouts: 0.83 us -> none  [per_device(): neighbour_table[:, :13]]
    pallas_call x1, Pallas kernels: 14.2 us -> 14.8 us  [per_device(): pl.pallas_call(conv_kernel, grid_spec=pltpu.PrefetchScalarGridSpec(num_sc...]
where the time goes in v4:
time: 50.2 us; the launch traced here: 49.8 us
  Pallas kernels  40.4 us (80%)
  local copies, waits for them, and re-layouts  6.19 us (12%)
  starting transfers between devices  2.31 us (5%)
  between operations  0.71 us (1%)
    pallas_call x1, Pallas kernels, per_device(): pl.pallas_call(exchange_kernel, in_specs=[smem, vmem], out_specs=[vmem] *...  24 us
    pallas_call x1, Pallas kernels, per_device(): pl.pallas_call(conv_kernel, grid_spec=pltpu.PrefetchScalarGridSpec(num_sc...  14.8 us
    unnamed x22, local copies, waits for them, and re-layouts  6.11 us
    ppermute x1, starting transfers between devices, swapped(): return lax.ppermute(block, axis, [(i, i ^ 1) for i in range(count)])  2.31 us
    pallas_call x1, Pallas kernels, per_device(): pl.pallas_call(place_kernel, in_specs=[smem, vmem, vmem, vmem], out_specs...  1.49 us
  transfers between devices with their start and end apart: 1, of which 0 were waited for; matrix products, arithmetic and copies ran while one was open for 1% of the time, Pallas kernels for 0%

profile of v4, /device:TPU:11, one launch (start us, length us, event | category | flops | bytes accessed | tf_op | source)
XLA Modules:
  0.0 49.8 jit_solution(5918283142938031794)
XLA Ops:
  0.6 0.0 copy-start
  0.6 1.2 %copy-done = bf16[8,512,128]{2,1,0:T(8,128)(2,1)S(1)} copy-done((bf16[8,512,128]{2,1,0:T(8,128)(2,1)S(1)}, bf16[8,512,128]{2,1,0:T(8,128)(2,1)}, u32[]{:S(2)}) %copy-start) | copy-done | bytes 1048600
  1.9 0.0 copy-start.3
  1.9 0.7 %copy-done.3 = s32[1,4,4]{2,1,0:T(4,128)S(1)} copy-done((s32[1,4,4]{2,1,0:T(4,128)S(1)}, s32[1,4,4]{2,1,0:T(4,128)}, u32[]{:S(2)}) %copy-start.3) | copy-done | bytes 88
  2.5 24.0 %shard_map.113 = (bf16[8,320,128]{2,1,0:T(8,128)(2,1)S(1)}, bf16[4,320,128]{2,1,0:T(8,128)(2,1)S(1)}, bf16[4,320,128]{2,1,0:T(8,128)(2,1)S(1)}, bf16[4,320,128]{2,1,0:T(8,128)(2,1)S(1)}, bf16[4,320,128]{2,1,0:T(8,128)(2,1)S(1)}) custom-call(s32[4,4]{1,0:T(4,128)S(1)} %bitcast.3, bf16[8,512,128]{2,1,0:T(8,128)(2,1)S(1)} %copy-done), custom_call_target="tpu_custom_call" | custom-call | bytes 60000000 | tf_op jit(solution)/shard_map/pallas_call | solution.py:259
  26.6 0.0 copy-start.6
  26.6 0.0 copy-start.7
  26.6 0.0 copy-start.8
  26.6 0.0 copy-done.1
  26.6 0.6 %copy-done.6 = s32[8,26]{1,0:T(8,128)S(1)} copy-done((s32[8,26]{1,0:T(8,128)S(1)}, s32[8,26]{1,0:T(8,128)}, u32[]{:S(2)}) %copy-start.6) | copy-done | bytes 856
  27.3 0.0 copy-done.7
  27.3 0.0 copy-done.8
  27.3 1.2 %copy-done.4 = bf16[3456,128]{1,0:T(8,128)(2,1)S(1)} copy-done((bf16[3456,128]{1,0:T(8,128)(2,1)S(1)}, bf16[3456,128]{1,0:T(8,128)(2,1)}, u32[]{:S(2)}) %copy-start.4) | copy-done | bytes 884760
  28.5 0.9 %copy-done.5 = bf16[1024,128]{1,0:T(8,128)(2,1)S(1)} copy-done((bf16[1024,128]{1,0:T(8,128)(2,1)S(1)}, bf16[1024,128]{1,0:T(8,128)(2,1)}, u32[]{:S(2)}) %copy-start.5) | copy-done | bytes 262168
  29.4 0.8 %copy-done.9 = bf16[128,128]{1,0:T(8,128)(2,1)S(1)} copy-done((bf16[128,128]{1,0:T(8,128)(2,1)S(1)}, bf16[128,128]{1,0:T(8,128)(2,1)}, u32[]{:S(2)}) %copy-start.9) | copy-done | bytes 32792
  30.2 14.8 %shard_map.114 = (bf16[8,512,128]{2,1,0:T(8,128)(2,1)}, bf16[8,64,128]{2,1,0:T(8,128)(2,1)S(1)}) custom-call(s32[8,26]{1,0:T(8,128)S(1)} %copy-done.6, bf16[8,512,128]{2,1,0:T(8,128)(2,1)S(1)} %copy-done.1, bf16[8,320,128]{2,1,0:T(8,128)(2,1)S(1)} %get-tuple-element.9.feats, bf16[4,320,128]{2,1,0:T(8,128)(2,1)S(1)} %get-tuple-element.10.from0, ...), custom_call_target="tpu_custom_call" | custom-call | flops 3623878656 | bytes 30000000 | tf_op jit(solution)/shard_map/pallas_call | solution.py:273
  45.0 2.3 %collective-permute-start = (bf16[8,64,128]{2,1,0:T(8,128)(2,1)S(1)}, bf16[8,64,128]{2,1,0:T(8,128)(2,1)S(1)}, u32[]{:S(2)}, u32[]{:S(2)}) collective-permute-start(bf16[8,64,128]{2,1,0:T(8,128)(2,1)S(1)} %get-tuple-element.15.mine), channel_id=1, source_target_pairs={{0,1},{1,0},{2,3},{3,2},{4,5},{5,4},{6,7},{7,6},{8,9},{9,8},{10,11... | collective-permute-start | bytes 393224 | tf_op jit(solution)/shard_map/ppermute | solution.py:14
  47.3 0.7 %copy-done.10 = s32[128]{0:T(128)S(1)} copy-done((s32[128]{0:T(128)S(1)}, s32[128]{0:T(128)}, u32[]{:S(2)}) %copy-start.10) | copy-done | bytes 536
  48.0 0.1 fusion
  48.1 0.1 pad_add_fusion
  48.1 0.2 select_reduce_fusion.source
  48.3 0.0 collective-permute-done.other
  48.3 0.0 copy-done.2
  48.3 1.5 %shard_map.115 = bf16[2,512,128]{2,1,0:T(8,128)(2,1)} custom-call(s32[16]{0:T(128)S(1)} %select_reduce_fusion.source, bf16[8,64,128]{2,1,0:T(8,128)(2,1)S(1)} %get-tuple-element.15.mine, bf16[8,64,128]{2,1,0:T(8,128)(2,1)S(1)} %collective-permute-done.other, bf16[64,64]{1,0:T(8,128)(2,1)S(1)} %copy-done.2), custom_call_target="tpu_custom_call" | custom-call | tf_op jit(solution)/shard_map/pallas_call | solution.py:317
  (6 shorter events, 0.0 us)
Async XLA Ops:
  0.6 1.2 %copy-start = (bf16[8,512,128]{2,1,0:T(8,128)(2,1)S(1)}, bf16[8,512,128]{2,1,0:T(8,128)(2,1)}, u32[]{:S(2)}) copy-start(bf16[8,512,128]{2,1,0:T(8,128)(2,1)} %own.1) | copy-start | bytes 3145732
  1.9 0.7 %copy-start.3 = (s32[1,4,4]{2,1,0:T(4,128)S(1)}, s32[1,4,4]{2,1,0:T(4,128)}, u32[]{:S(2)}) copy-start(s32[1,4,4]{2,1,0:T(4,128)} %param.12) | copy-start | bytes 196
  2.5 24.1 %copy-start.1 = (bf16[8,512,128]{2,1,0:T(8,128)(2,1)S(1)}, bf16[8,512,128]{2,1,0:T(8,128)(2,1)}, u32[]{:S(2)}) copy-start(bf16[8,512,128]{2,1,0:T(8,128)(2,1)} %own.1) | copy-start | bytes 3145732
  26.6 0.7 %copy-start.6 = (s32[8,26]{1,0:T(8,128)S(1)}, s32[8,26]{1,0:T(8,128)}, u32[]{:S(2)}) copy-start(s32[8,26]{1,0:T(8,128)} %ids.1) | copy-start | bytes 2500
  26.6 0.7 %copy-start.7 = (f32[128]{0:T(128)S(1)}, f32[128]{0:T(128)}, u32[]{:S(2)}) copy-start(f32[128]{0:T(128)} %param.15) | copy-start | bytes 1540
  26.6 0.7 %copy-start.8 = (f32[128]{0:T(128)S(1)}, f32[128]{0:T(128)}, u32[]{:S(2)}) copy-start(f32[128]{0:T(128)} %param.16) | copy-start | bytes 1540
  27.3 1.2 %copy-start.4 = (bf16[3456,128]{1,0:T(8,128)(2,1)S(1)}, bf16[3456,128]{1,0:T(8,128)(2,1)}, u32[]{:S(2)}) copy-start(bf16[3456,128]{1,0:T(8,128)(2,1)} %weight.1) | copy-start | bytes 2654212
  28.5 0.9 %copy-start.5 = (bf16[1024,128]{1,0:T(8,128)(2,1)S(1)}, bf16[1024,128]{1,0:T(8,128)(2,1)}, u32[]{:S(2)}) copy-start(bf16[1024,128]{1,0:T(8,128)(2,1)} %reduce.1) | copy-start | bytes 786436
  29.4 0.8 %copy-start.9 = (bf16[128,128]{1,0:T(8,128)(2,1)S(1)}, bf16[128,128]{1,0:T(8,128)(2,1)}, u32[]{:S(2)}) copy-start(bf16[128,128]{1,0:T(8,128)(2,1)} %constant.32.clone.order) | copy-start | bytes 98308
  45.0 3.3 %collective-permute-start = (bf16[8,64,128]{2,1,0:T(8,128)(2,1)S(1)}, bf16[8,64,128]{2,1,0:T(8,128)(2,1)S(1)}, u32[]{:S(2)}, u32[]{:S(2)}) collective-permute-start(bf16[8,64,128]{2,1,0:T(8,128)(2,1)S(1)} %get-tuple-element.15.mine), channel_id=1, source_target_pairs={{0,1},{1,0},{2,3},{3,2},{4,5},{5,4},{6,7},{7,6},{8,9},{9,8},{10,11... | collective-permute-start | bytes 393224 | tf_op jit(solution)/shard_map/ppermute | solution.py:14
  47.3 1.0 %copy-start.2 = (bf16[64,64]{1,0:T(8,128)(2,1)S(1)}, bf16[64,64]{1,0:T(8,128)(2,1)}, u32[]{:S(2)}) copy-start(bf16[64,64]{1,0:T(8,128)(2,1)} %constant.33.clone.order) | copy-start | bytes 24580
  47.3 0.7 %copy-start.10 = (s32[128]{0:T(128)S(1)}, s32[128]{0:T(128)}, u32[]{:S(2)}) copy-start(s32[128]{0:T(128)} %param.13) | copy-start | bytes 1540

commit v5 on v3

--- a/solution.py
+++ b/solution.py
@@ -105,7 +105,7 @@
     z = lax.broadcasted_iota(jnp.int32, (8, 8, 128), 1)
 
     def rows_of(number, start, size):
-        return ext[ids[g, number], start : start + size].astype(jnp.float32)
+        return ext[ids[g, number - (number > 13)], start : start + size].astype(jnp.float32)
 
     def spread(line):
         return jnp.broadcast_to(line[:, None, :], (8, 8, 128))
@@ -206,14 +206,34 @@
             order[...], out[a * 128 : (a + 1) * 128], preferred_element_type=jnp.float32
         ).astype(jnp.bfloat16)
         for p in range(8):
-            grouped[a * 16 : (a + 1) * 16, p * 128 : (p + 1) * 128] = rows[p * 16 : (p + 1) * 16]
-    octant[0] = jnp.dot(
-        grouped[...], reduce[...], preferred_element_type=jnp.float32
-    ).astype(jnp.bfloat16)
-
-
-def place_kernel(source, mine, other, order, coarse, rows, stack):
-    count = mine.shape[0]
+            grouped[g, a * 16 : (a + 1) * 16, p * 128 : (p + 1) * 128] = rows[p * 16 : (p + 1) * 16]
+
+    @pl.when(g == blocks - 1)
+    def _():
+        octant[...] = (
+            jnp.dot(
+                grouped[...].reshape(blocks * 64, 1024),
+                reduce[...],
+                preferred_element_type=jnp.float32,
+            )
+            .astype(jnp.bfloat16)
+            .reshape(octant.shape)
+        )
+
+
+def place_kernel(targets, mine, other, order, coarse, rows, stack, source):
+    count, octants = mine.shape[0], 8 * coarse.shape[0]
+    me = lax.axis_index("cell")
+    for i in range(octants):
+        source[i] = 2 * count
+    for part, device in enumerate((me, me + 1 - 2 * (me % 2))):
+        for i in range(count):
+            place = targets[device * count + i] - (me % 2) * octants
+
+            @pl.when((place >= 0) & (place < octants))
+            def _(place=place, row=part * count + i):
+                source[place] = row
+
     rows[:count] = mine[...]
     rows[count : 2 * count] = other[...]
     rows[2 * count] = jnp.zeros(rows.shape[1:], rows.dtype)
@@ -243,7 +263,6 @@
     blocks = features.shape[0]
     slots = send_lists.shape[2]
     channels = features.shape[2]
-    myself = lax.axis_index("cell")
     vmem = pl.BlockSpec(memory_space=pltpu.VMEM)
     smem = pl.BlockSpec(memory_space=pltpu.SMEM)
     hbm = pl.BlockSpec(memory_space=pl.ANY)
@@ -261,8 +280,6 @@
             vmem_limit_bytes=24 * 1024 * 1024, collective_id=0, has_side_effects=True
         ),
     )(send_lists[0], features)
-    self_id = jnp.arange(blocks, dtype=jnp.int32)[:, None]
-    ids = jnp.concatenate([neighbour_table[:, :13], self_id, neighbour_table[:, 13:]], axis=1)
     fine, octants = pl.pallas_call(
         conv_kernel,
         grid_spec=pltpu.PrefetchScalarGridSpec(
@@ -271,12 +288,12 @@
             in_specs=[vmem] + [hbm] * 5 + [vmem] * 5,
             out_specs=[
                 pl.BlockSpec((1, 512, channels), lambda g, ids: (g, 0, 0)),
-                pl.BlockSpec((1, 64, channels), lambda g, ids: (g, 0, 0)),
+                pl.BlockSpec((blocks, 64, channels), lambda g, ids: (0, 0, 0)),
             ],
             scratch_shapes=[
                 pltpu.VMEM((blocks + 4 * slots + 1, rows, channels), jnp.bfloat16),
                 pltpu.VMEM((10, 64, 9 * channels), jnp.bfloat16),
-                pltpu.VMEM((64, 8 * channels), jnp.bfloat16),
+                pltpu.VMEM((blocks, 64, 8 * channels), jnp.bfloat16),
                 pltpu.SemaphoreType.DMA((5,)),
             ],
         ),
@@ -286,21 +303,11 @@
         ],
         compiler_params=pltpu.CompilerParams(vmem_limit_bytes=40 * 1024 * 1024),
     )(
-        ids, features, shell, *received, conv_weight, norm_gain[None], norm_shift[None],
+        neighbour_table, features, shell, *received, conv_weight, norm_gain[None], norm_shift[None],
         reduce_weight_matrix, octant_order(),
     )
     partner_octants = swapped(octants, "cell")
-    partner = jnp.bitwise_xor(myself, 1)
-    targets = jnp.concatenate(
-        [
-            lax.dynamic_slice_in_dim(coarse_target, myself * blocks, blocks),
-            lax.dynamic_slice_in_dim(coarse_target, partner * blocks, blocks),
-        ]
-    )
     coarse_slots = blocks // 4
-    wanted = (myself % 2) * 8 * coarse_slots + jnp.arange(8 * coarse_slots, dtype=jnp.int32)
-    hit = targets[None, :] == wanted[:, None]
-    source = jnp.min(jnp.where(hit, jnp.arange(2 * blocks, dtype=jnp.int32), 2 * blocks), axis=1)
     coarse = pl.pallas_call(
         place_kernel,
         in_specs=[smem, vmem, vmem, vmem],
@@ -309,9 +316,10 @@
         scratch_shapes=[
             pltpu.VMEM((2 * blocks + 1, 64, channels), jnp.bfloat16),
             pltpu.VMEM((64, channels), jnp.bfloat16),
+            pltpu.SMEM((8 * coarse_slots,), jnp.int32),
         ],
         compiler_params=pltpu.CompilerParams(vmem_limit_bytes=16 * 1024 * 1024),
-    )(source.astype(jnp.int32), octants, partner_octants, coarse_order())
+    )(coarse_target, octants, partner_octants, coarse_order())
     return (fine, coarse)
 
 

time: 49 us -> 48.7 us (level)
  waiting for transfers between devices: 0.01 us -> 0.99 us
  Pallas kernels: 39.7 us -> 38.9 us
    ppermute x1, waiting for transfers between devices: 0.01 us -> 0.99 us  [swapped(): return lax.ppermute(block, axis, [(i, i ^ 1) for i in range(count)])]
    slice x1 -> x0, local copies, waits for them, and re-layouts: 0.83 us -> none  [per_device(): neighbour_table[:, :13]]
    pallas_call x1, Pallas kernels: 14.2 us -> 13.4 us  [per_device(): pl.pallas_call(conv_kernel, grid_spec=pltpu.PrefetchScalarGridSpec(num_sc...]
    unnamed x20 -> x22, local copies, waits for them, and re-layouts: 4.69 us -> 5.45 us
  transfers between devices with their start and end apart: 1 -> 1, of which waited for: 0 -> 1; matrix products, arithmetic and copies ran while one was open for 1% -> 0% of each run, Pallas kernels for 0% -> 0%
where the time goes in v5:
time: 48.7 us; the launch traced here: 48.4 us
  Pallas kernels  38.9 us (80%)
  local copies, waits for them, and re-layouts  5.45 us (11%)
  starting transfers between devices  2.32 us (5%)
  waiting for transfers between devices  0.99 us (2%)
  between operations  0.7 us (1%)
    pallas_call x1, Pallas kernels, per_device(): pl.pallas_call(exchange_kernel, in_specs=[smem, vmem], out_specs=[vmem] *...  24 us
    pallas_call x1, Pallas kernels, per_device(): pl.pallas_call(conv_kernel, grid_spec=pltpu.PrefetchScalarGridSpec(num_sc...  13.4 us
    unnamed x22, local copies, waits for them, and re-layouts  5.45 us
    ppermute x1, starting transfers between devices, swapped(): return lax.ppermute(block, axis, [(i, i ^ 1) for i in range(count)])  2.32 us
    pallas_call x1, Pallas kernels, per_device(): pl.pallas_call(place_kernel, in_specs=[smem, vmem, vmem, vmem], out_specs...  1.53 us
    ppermute x1, waiting for transfers between devices, swapped(): return lax.ppermute(block, axis, [(i, i ^ 1) for i in range(count)])  0.99 us
  transfers between devices with their start and end apart: 1, of which 1 were waited for; matrix products, arithmetic and copies ran while one was open for 0% of the time, Pallas kernels for 0%

profile of v5, /device:TPU:11, one launch (start us, length us, event | category | flops | bytes accessed | tf_op | source)
XLA Modules:
  0.0 48.4 jit_solution(1939218229638588696)
XLA Ops:
  0.6 0.0 copy-start
  0.6 1.2 %copy-done = bf16[8,512,128]{2,1,0:T(8,128)(2,1)S(1)} copy-done((bf16[8,512,128]{2,1,0:T(8,128)(2,1)S(1)}, bf16[8,512,128]{2,1,0:T(8,128)(2,1)}, u32[]{:S(2)}) %copy-start) | copy-done | bytes 1048600
  1.9 0.0 copy-start.7
  1.9 0.7 %copy-done.7 = s32[1,4,4]{2,1,0:T(4,128)S(1)} copy-done((s32[1,4,4]{2,1,0:T(4,128)S(1)}, s32[1,4,4]{2,1,0:T(4,128)}, u32[]{:S(2)}) %copy-start.7) | copy-done | bytes 88
  2.5 0.0 copy-start.1
  2.5 24.0 %shard_map.113 = (bf16[8,320,128]{2,1,0:T(8,128)(2,1)S(1)}, bf16[4,320,128]{2,1,0:T(8,128)(2,1)S(1)}, bf16[4,320,128]{2,1,0:T(8,128)(2,1)S(1)}, bf16[4,320,128]{2,1,0:T(8,128)(2,1)S(1)}, bf16[4,320,128]{2,1,0:T(8,128)(2,1)S(1)}) custom-call(s32[4,4]{1,0:T(4,128)S(1)} %bitcast.3, bf16[8,512,128]{2,1,0:T(8,128)(2,1)S(1)} %copy-done), custom_call_target="tpu_custom_call" | custom-call | tf_op jit(solution)/shard_map/pallas_call | solution.py:270
  26.6 0.0 copy-start.6
  26.6 0.0 copy-start.9
  26.6 0.0 copy-start.10
  26.6 0.0 copy-done.1
  26.6 0.6 %copy-done.6 = s32[8,26]{1,0:T(8,128)S(1)} copy-done((s32[8,26]{1,0:T(8,128)S(1)}, s32[8,26]{1,0:T(8,128)}, u32[]{:S(2)}) %copy-start.6) | copy-done | bytes 856
  27.3 0.0 copy-done.9
  27.3 0.0 copy-done.10
  27.3 0.0 copy-start.2
  27.3 1.2 %copy-done.2 = bf16[3456,128]{1,0:T(8,128)(2,1)S(1)} copy-done((bf16[3456,128]{1,0:T(8,128)(2,1)S(1)}, bf16[3456,128]{1,0:T(8,128)(2,1)}, u32[]{:S(2)}) %copy-start.2) | copy-done | bytes 884760
  28.5 0.9 %copy-done.3 = bf16[1024,128]{1,0:T(8,128)(2,1)S(1)} copy-done((bf16[1024,128]{1,0:T(8,128)(2,1)S(1)}, bf16[1024,128]{1,0:T(8,128)(2,1)}, u32[]{:S(2)}) %copy-start.3) | copy-done | bytes 262168
  29.4 0.8 %copy-done.4 = bf16[128,128]{1,0:T(8,128)(2,1)S(1)} copy-done((bf16[128,128]{1,0:T(8,128)(2,1)S(1)}, bf16[128,128]{1,0:T(8,128)(2,1)}, u32[]{:S(2)}) %copy-start.4) | copy-done | bytes 32792
  30.2 13.4 %shard_map.114 = (bf16[8,512,128]{2,1,0:T(8,128)(2,1)}, bf16[8,64,128]{2,1,0:T(8,128)(2,1)S(1)}) custom-call(s32[8,26]{1,0:T(8,128)S(1)} %copy-done.6, bf16[8,512,128]{2,1,0:T(8,128)(2,1)S(1)} %copy-done.1, bf16[8,320,128]{2,1,0:T(8,128)(2,1)S(1)} %get-tuple-element.9.feats, bf16[4,320,128]{2,1,0:T(8,128)(2,1)S(1)} %get-tuple-element.10.from0, ...), custom_call_target="tpu_custom_call" | custom-call | tf_op jit(solution)/shard_map/pallas_call | solution.py:283
  43.5 0.0 copy-start.8
  43.6 2.3 %collective-permute-start = (bf16[8,64,128]{2,1,0:T(8,128)(2,1)S(1)}, bf16[8,64,128]{2,1,0:T(8,128)(2,1)S(1)}, u32[]{:S(2)}, u32[]{:S(2)}) collective-permute-start(bf16[8,64,128]{2,1,0:T(8,128)(2,1)S(1)} %get-tuple-element.15.mine), channel_id=1, source_target_pairs={{0,1},{1,0},{2,3},{3,2},{4,5},{5,4},{6,7},{7,6},{8,9},{9,8},{10,11... | collective-permute-start | bytes 393224 | tf_op jit(solution)/shard_map/ppermute | solution.py:14
  45.9 1.0 %collective-permute-done.other = bf16[8,64,128]{2,1,0:T(8,128)(2,1)S(1)} collective-permute-done((bf16[8,64,128]{2,1,0:T(8,128)(2,1)S(1)}, bf16[8,64,128]{2,1,0:T(8,128)(2,1)S(1)}, u32[]{:S(2)}, u32[]{:S(2)}) %collective-permute-start) | collective-permute-done | bytes 131104 | tf_op jit(solution)/shard_map/ppermute | solution.py:14
  46.9 0.0 copy-done.5
  46.9 0.0 copy-done.8
  46.9 1.5 %shard_map.115 = bf16[2,512,128]{2,1,0:T(8,128)(2,1)} custom-call(s32[128]{0:T(128)S(1)} %copy-done.8, bf16[8,64,128]{2,1,0:T(8,128)(2,1)S(1)} %get-tuple-element.15.mine, bf16[8,64,128]{2,1,0:T(8,128)(2,1)S(1)} %collective-permute-done.other, bf16[64,64]{1,0:T(8,128)(2,1)S(1)} %copy-done.5), custom_call_target="tpu_custom_call" | custom-call | tf_op jit(solution)/shard_map/pallas_call | solution.py:311
  (3 shorter events, 0.0 us)
Async XLA Ops:
  0.6 1.2 %copy-start = (bf16[8,512,128]{2,1,0:T(8,128)(2,1)S(1)}, bf16[8,512,128]{2,1,0:T(8,128)(2,1)}, u32[]{:S(2)}) copy-start(bf16[8,512,128]{2,1,0:T(8,128)(2,1)} %own.1) | copy-start | bytes 3145732
  1.9 0.7 %copy-start.7 = (s32[1,4,4]{2,1,0:T(4,128)S(1)}, s32[1,4,4]{2,1,0:T(4,128)}, u32[]{:S(2)}) copy-start(s32[1,4,4]{2,1,0:T(4,128)} %param.12) | copy-start | bytes 196
  2.5 24.1 %copy-start.1 = (bf16[8,512,128]{2,1,0:T(8,128)(2,1)S(1)}, bf16[8,512,128]{2,1,0:T(8,128)(2,1)}, u32[]{:S(2)}) copy-start(bf16[8,512,128]{2,1,0:T(8,128)(2,1)} %own.1) | copy-start | bytes 3145732
  26.6 0.7 %copy-start.6 = (s32[8,26]{1,0:T(8,128)S(1)}, s32[8,26]{1,0:T(8,128)}, u32[]{:S(2)}) copy-start(s32[8,26]{1,0:T(8,128)} %ids.1) | copy-start | bytes 2500
  26.6 0.7 %copy-start.9 = (f32[128]{0:T(128)S(1)}, f32[128]{0:T(128)}, u32[]{:S(2)}) copy-start(f32[128]{0:T(128)} %param.15) | copy-start | bytes 1540
  26.6 0.7 %copy-start.10 = (f32[128]{0:T(128)S(1)}, f32[128]{0:T(128)}, u32[]{:S(2)}) copy-start(f32[128]{0:T(128)} %param.16) | copy-start | bytes 1540
  27.3 1.2 %copy-start.2 = (bf16[3456,128]{1,0:T(8,128)(2,1)S(1)}, bf16[3456,128]{1,0:T(8,128)(2,1)}, u32[]{:S(2)}) copy-start(bf16[3456,128]{1,0:T(8,128)(2,1)} %weight.1) | copy-start | bytes 2654212
  28.5 0.9 %copy-start.3 = (bf16[1024,128]{1,0:T(8,128)(2,1)S(1)}, bf16[1024,128]{1,0:T(8,128)(2,1)}, u32[]{:S(2)}) copy-start(bf16[1024,128]{1,0:T(8,128)(2,1)} %reduce.1) | copy-start | bytes 786436
  29.4 0.8 %copy-start.4 = (bf16[128,128]{1,0:T(8,128)(2,1)S(1)}, bf16[128,128]{1,0:T(8,128)(2,1)}, u32[]{:S(2)}) copy-start(bf16[128,128]{1,0:T(8,128)(2,1)} %constant.4.clone.order) | copy-start | bytes 98308
  30.2 16.7 %copy-start.5 = (bf16[64,64]{1,0:T(8,128)(2,1)S(1)}, bf16[64,64]{1,0:T(8,128)(2,1)}, u32[]{:S(2)}) copy-start(bf16[64,64]{1,0:T(8,128)(2,1)} %constant.5.clone.order) | copy-start | bytes 24580
  43.5 3.3 %copy-start.8 = (s32[128]{0:T(128)S(1)}, s32[128]{0:T(128)}, u32[]{:S(2)}) copy-start(s32[128]{0:T(128)} %targets.1) | copy-start | bytes 1540
  43.6 3.3 %collective-permute-start = (bf16[8,64,128]{2,1,0:T(8,128)(2,1)S(1)}, bf16[8,64,128]{2,1,0:T(8,128)(2,1)S(1)}, u32[]{:S(2)}, u32[]{:S(2)}) collective-permute-start(bf16[8,64,128]{2,1,0:T(8,128)(2,1)S(1)} %get-tuple-element.15.mine), channel_id=1, source_target_pairs={{0,1},{1,0},{2,3},{3,2},{4,5},{5,4},{6,7},{7,6},{8,9},{9,8},{10,11... | collective-permute-start | bytes 393224 | tf_op jit(solution)/shard_map/ppermute | solution.py:14

commit v6 on v5

--- a/solution.py
+++ b/solution.py
@@ -15,13 +15,12 @@
 
 
 def octant_order():
-    order = np.zeros((128, 128), np.float32)
-    for p in range(8):
-        px, py, pz = p // 4, p // 2 % 2, p % 2
-        for b in range(4):
-            for c in range(4):
-                order[p * 16 + b * 4 + c, px * 64 + (2 * b + py) * 8 + 2 * c + pz] = 1
-    return jnp.asarray(order, jnp.bfloat16)
+    r = lax.broadcasted_iota(jnp.int32, (128, 128), 0)
+    column = lax.broadcasted_iota(jnp.int32, (128, 128), 1)
+    px, py, pz = r >> 6, (r >> 5) & 1, (r >> 4) & 1
+    b, c = (r >> 2) & 3, r & 3
+    hit = column == px * 64 + (2 * b + py) * 8 + 2 * c + pz
+    return jnp.where(hit, 1.0, 0.0).astype(jnp.bfloat16)
 
 
 def coarse_order():
@@ -169,8 +168,8 @@
 
 
 def conv_kernel(
-    ids, own, feats, from0, from1, from2, from3, weight, gain, shift, reduce, order,
-    fine, octant, ext, cols, grouped, sems,
+    ids, own, feats, from0, from1, from2, from3, weight, gain, shift, reduce,
+    fine, octant, ext, cols, grouped, order, sems,
 ):
     g = pl.program_id(0)
     blocks, slots = feats.shape[0], from0.shape[0]
@@ -186,6 +185,7 @@
             )
         for copy in copies:
             copy.start()
+        order[...] = octant_order()
         ext[blocks + 4 * slots] = jnp.zeros(ext.shape[1:], ext.dtype)
         for copy in copies:
             copy.wait()
@@ -285,7 +285,7 @@
         grid_spec=pltpu.PrefetchScalarGridSpec(
             num_scalar_prefetch=1,
             grid=(blocks,),
-            in_specs=[vmem] + [hbm] * 5 + [vmem] * 5,
+            in_specs=[vmem] + [hbm] * 5 + [vmem] * 4,
             out_specs=[
                 pl.BlockSpec((1, 512, channels), lambda g, ids: (g, 0, 0)),
                 pl.BlockSpec((blocks, 64, channels), lambda g, ids: (0, 0, 0)),
@@ -294,6 +294,7 @@
                 pltpu.VMEM((blocks + 4 * slots + 1, rows, channels), jnp.bfloat16),
                 pltpu.VMEM((10, 64, 9 * channels), jnp.bfloat16),
                 pltpu.VMEM((blocks, 64, 8 * channels), jnp.bfloat16),
+                pltpu.VMEM((128, 128), jnp.bfloat16),
                 pltpu.SemaphoreType.DMA((5,)),
             ],
         ),
@@ -304,7 +305,7 @@
         compiler_params=pltpu.CompilerParams(vmem_limit_bytes=40 * 1024 * 1024),
     )(
         neighbour_table, features, shell, *received, conv_weight, norm_gain[None], norm_shift[None],
-        reduce_weight_matrix, octant_order(),
+        reduce_weight_matrix,
     )
     partner_octants = swapped(octants, "cell")
     coarse_slots = blocks // 4

time: 48.7 us -> 48 us (0.986)
  local copies, waits for them, and re-layouts: 5.45 us -> 4.69 us
    unnamed x22 -> x20, local copies, waits for them, and re-layouts: 5.45 us -> 4.69 us
where the time goes in v6:
time: 48 us; the launch traced here: 47.7 us
  Pallas kernels  39 us (81%)
  local copies, waits for them, and re-layouts  4.69 us (10%)
  starting transfers between devices  2.32 us (5%)
  waiting for transfers between devices  0.99 us (2%)
  between operations  0.7 us (1%)
    pallas_call x1, Pallas kernels, per_device(): pl.pallas_call(exchange_kernel, in_specs=[smem, vmem], out_specs=[vmem] *...  24 us
    pallas_call x1, Pallas kernels, per_device(): pl.pallas_call(conv_kernel, grid_spec=pltpu.PrefetchScalarGridSpec(num_sc...  13.4 us
    unnamed x20, local copies, waits for them, and re-layouts  4.69 us
    ppermute x1, starting transfers between devices, swapped(): return lax.ppermute(block, axis, [(i, i ^ 1) for i in range(count)])  2.32 us
    pallas_call x1, Pallas kernels, per_device(): pl.pallas_call(place_kernel, in_specs=[smem, vmem, vmem, vmem], out_specs...  1.53 us
    ppermute x1, waiting for transfers between devices, swapped(): return lax.ppermute(block, axis, [(i, i ^ 1) for i in range(count)])  0.99 us
  transfers between devices with their start and end apart: 1, of which 1 were waited for; matrix products, arithmetic and copies ran while one was open for 0% of the time, Pallas kernels for 0%

profile of v6, /device:TPU:11, one launch (start us, length us, event | category | flops | bytes accessed | tf_op | source)
XLA Modules:
  0.0 47.7 jit_solution(15612833504576264755)
XLA Ops:
  0.6 0.0 copy-start
  0.6 1.2 %copy-done = bf16[8,512,128]{2,1,0:T(8,128)(2,1)S(1)} copy-done((bf16[8,512,128]{2,1,0:T(8,128)(2,1)S(1)}, bf16[8,512,128]{2,1,0:T(8,128)(2,1)}, u32[]{:S(2)}) %copy-start) | copy-done | bytes 1048600
  1.9 0.7 %copy-done.6 = s32[1,4,4]{2,1,0:T(4,128)S(1)} copy-done((s32[1,4,4]{2,1,0:T(4,128)S(1)}, s32[1,4,4]{2,1,0:T(4,128)}, u32[]{:S(2)}) %copy-start.6) | copy-done | bytes 88
  2.5 0.0 copy-start.1
  2.5 24.0 %shard_map.104 = (bf16[8,320,128]{2,1,0:T(8,128)(2,1)S(1)}, bf16[4,320,128]{2,1,0:T(8,128)(2,1)S(1)}, bf16[4,320,128]{2,1,0:T(8,128)(2,1)S(1)}, bf16[4,320,128]{2,1,0:T(8,128)(2,1)S(1)}, bf16[4,320,128]{2,1,0:T(8,128)(2,1)S(1)}) custom-call(s32[4,4]{1,0:T(4,128)S(1)} %bitcast.3, bf16[8,512,128]{2,1,0:T(8,128)(2,1)S(1)} %copy-done), custom_call_target="tpu_custom_call" | custom-call | tf_op jit(solution)/shard_map/pallas_call | solution.py:270
  26.6 0.0 copy-start.5
  26.6 0.0 copy-start.8
  26.6 0.0 copy-start.9
  26.6 0.0 copy-done.1
  26.6 0.6 %copy-done.5 = s32[8,26]{1,0:T(8,128)S(1)} copy-done((s32[8,26]{1,0:T(8,128)S(1)}, s32[8,26]{1,0:T(8,128)}, u32[]{:S(2)}) %copy-start.5) | copy-done | bytes 856
  27.3 0.0 copy-done.8
  27.3 0.0 copy-done.9
  27.3 0.0 copy-start.2
  27.3 1.2 %copy-done.2 = bf16[3456,128]{1,0:T(8,128)(2,1)S(1)} copy-done((bf16[3456,128]{1,0:T(8,128)(2,1)S(1)}, bf16[3456,128]{1,0:T(8,128)(2,1)}, u32[]{:S(2)}) %copy-start.2) | copy-done | bytes 884760
  28.5 0.0 copy-start.3
  28.5 0.9 %copy-done.3 = bf16[1024,128]{1,0:T(8,128)(2,1)S(1)} copy-done((bf16[1024,128]{1,0:T(8,128)(2,1)S(1)}, bf16[1024,128]{1,0:T(8,128)(2,1)}, u32[]{:S(2)}) %copy-start.3) | copy-done | bytes 262168
  29.4 0.0 copy-start.4
  29.4 13.4 %shard_map.105 = (bf16[8,512,128]{2,1,0:T(8,128)(2,1)}, bf16[8,64,128]{2,1,0:T(8,128)(2,1)S(1)}) custom-call(s32[8,26]{1,0:T(8,128)S(1)} %copy-done.5, bf16[8,512,128]{2,1,0:T(8,128)(2,1)S(1)} %copy-done.1, bf16[8,320,128]{2,1,0:T(8,128)(2,1)S(1)} %get-tuple-element.9.feats, bf16[4,320,128]{2,1,0:T(8,128)(2,1)S(1)} %get-tuple-element.10.from0, ...), custom_call_target="tpu_custom_call" | custom-call | tf_op jit(solution)/shard_map/pallas_call | solution.py:283
  42.8 0.0 copy-start.7
  42.8 2.3 %collective-permute-start = (bf16[8,64,128]{2,1,0:T(8,128)(2,1)S(1)}, bf16[8,64,128]{2,1,0:T(8,128)(2,1)S(1)}, u32[]{:S(2)}, u32[]{:S(2)}) collective-permute-start(bf16[8,64,128]{2,1,0:T(8,128)(2,1)S(1)} %get-tuple-element.15.mine), channel_id=1, source_target_pairs={{0,1},{1,0},{2,3},{3,2},{4,5},{5,4},{6,7},{7,6},{8,9},{9,8},{10,11... | collective-permute-start | bytes 393224 | tf_op jit(solution)/shard_map/ppermute | solution.py:14
  45.2 1.0 %collective-permute-done.other = bf16[8,64,128]{2,1,0:T(8,128)(2,1)S(1)} collective-permute-done((bf16[8,64,128]{2,1,0:T(8,128)(2,1)S(1)}, bf16[8,64,128]{2,1,0:T(8,128)(2,1)S(1)}, u32[]{:S(2)}, u32[]{:S(2)}) %collective-permute-start) | collective-permute-done | bytes 131104 | tf_op jit(solution)/shard_map/ppermute | solution.py:14
  46.1 0.0 copy-done.4
  46.1 0.0 copy-done.7
  46.1 1.5 %shard_map.106 = bf16[2,512,128]{2,1,0:T(8,128)(2,1)} custom-call(s32[128]{0:T(128)S(1)} %copy-done.7, bf16[8,64,128]{2,1,0:T(8,128)(2,1)S(1)} %get-tuple-element.15.mine, bf16[8,64,128]{2,1,0:T(8,128)(2,1)S(1)} %collective-permute-done.other, bf16[64,64]{1,0:T(8,128)(2,1)S(1)} %copy-done.4), custom_call_target="tpu_custom_call" | custom-call | tf_op jit(solution)/shard_map/pallas_call | solution.py:312
  (1 shorter events, 0.0 us)
Async XLA Ops:
  0.6 1.2 %copy-start = (bf16[8,512,128]{2,1,0:T(8,128)(2,1)S(1)}, bf16[8,512,128]{2,1,0:T(8,128)(2,1)}, u32[]{:S(2)}) copy-start(bf16[8,512,128]{2,1,0:T(8,128)(2,1)} %own.1) | copy-start | bytes 3145732
  1.9 0.7 %copy-start.6 = (s32[1,4,4]{2,1,0:T(4,128)S(1)}, s32[1,4,4]{2,1,0:T(4,128)}, u32[]{:S(2)}) copy-start(s32[1,4,4]{2,1,0:T(4,128)} %param.11) | copy-start | bytes 196
  2.5 24.1 %copy-start.1 = (bf16[8,512,128]{2,1,0:T(8,128)(2,1)S(1)}, bf16[8,512,128]{2,1,0:T(8,128)(2,1)}, u32[]{:S(2)}) copy-start(bf16[8,512,128]{2,1,0:T(8,128)(2,1)} %own.1) | copy-start | bytes 3145732
  26.6 0.7 %copy-start.5 = (s32[8,26]{1,0:T(8,128)S(1)}, s32[8,26]{1,0:T(8,128)}, u32[]{:S(2)}) copy-start(s32[8,26]{1,0:T(8,128)} %ids.1) | copy-start | bytes 2500
  26.6 0.7 %copy-start.8 = (f32[128]{0:T(128)S(1)}, f32[128]{0:T(128)}, u32[]{:S(2)}) copy-start(f32[128]{0:T(128)} %param.14) | copy-start | bytes 1540
  26.6 0.7 %copy-start.9 = (f32[128]{0:T(128)S(1)}, f32[128]{0:T(128)}, u32[]{:S(2)}) copy-start(f32[128]{0:T(128)} %param.15) | copy-start | bytes 1540
  27.3 1.2 %copy-start.2 = (bf16[3456,128]{1,0:T(8,128)(2,1)S(1)}, bf16[3456,128]{1,0:T(8,128)(2,1)}, u32[]{:S(2)}) copy-start(bf16[3456,128]{1,0:T(8,128)(2,1)} %weight.1) | copy-start | bytes 2654212
  28.5 0.9 %copy-start.3 = (bf16[1024,128]{1,0:T(8,128)(2,1)S(1)}, bf16[1024,128]{1,0:T(8,128)(2,1)}, u32[]{:S(2)}) copy-start(bf16[1024,128]{1,0:T(8,128)(2,1)} %reduce.1) | copy-start | bytes 786436
  29.4 16.7 %copy-start.4 = (bf16[64,64]{1,0:T(8,128)(2,1)S(1)}, bf16[64,64]{1,0:T(8,128)(2,1)}, u32[]{:S(2)}) copy-start(bf16[64,64]{1,0:T(8,128)(2,1)} %constant.2.clone.order) | copy-start | bytes 24580
  42.8 3.3 %copy-start.7 = (s32[128]{0:T(128)S(1)}, s32[128]{0:T(128)}, u32[]{:S(2)}) copy-start(s32[128]{0:T(128)} %targets.1) | copy-start | bytes 1540
  42.8 3.3 %collective-permute-start = (bf16[8,64,128]{2,1,0:T(8,128)(2,1)S(1)}, bf16[8,64,128]{2,1,0:T(8,128)(2,1)S(1)}, u32[]{:S(2)}, u32[]{:S(2)}) collective-permute-start(bf16[8,64,128]{2,1,0:T(8,128)(2,1)S(1)} %get-tuple-element.15.mine), channel_id=1, source_target_pairs={{0,1},{1,0},{2,3},{3,2},{4,5},{5,4},{6,7},{7,6},{8,9},{9,8},{10,11... | collective-permute-start | bytes 393224 | tf_op jit(solution)/shard_map/ppermute | solution.py:14
